TPU v7x, 32 devices: a whole 2x2x4 slice. The times are simulated.
32 devices in a mesh: dp: 16 (over z, y, x), mp: 2 (over core).
Axes of the slice: x: 2, y: 2, z: 4, core: 2. Of those that a mesh axis runs over, the one named last changes fastest.
Arguments:
- dec_input: bfloat16 [16, 512, 768], P('dp'), may hold values from -6 to 6
- out_grad: bfloat16 [16, 512, 768], P('dp'), may hold values from -8 to 8
- enc_feats: bfloat16 [16, 2, 16, 128, 768], P('dp', 'mp'), may hold values from -16 to 16
- mem_lengths: int32 [16], replicated, may hold values from 256 to 4096, as said below
- dec_lengths: int32 [16], replicated, may hold values from 128 to 512, as said below
- doc_owner: int32 [16], replicated, may hold values from 0 to 15, each once
- group_gain: float32 [768], replicated, may hold values from 0.5 to 1.5
- group_bias: float32 [768], replicated, may hold values from -3 to 3
- conv_weight: bfloat16 [768, 768], replicated, may hold values from -0.21875 to 0.21875
- cross_kv: bfloat16 [768, 2, 768], replicated, may hold values from -0.21875 to 0.21875
- self_gain: float32 [768], replicated, may hold values from 0.5 to 1.5
- self_qkv: bfloat16 [768, 3, 768], P(None, None, 'mp'), may hold values from -0.21875 to 0.21875
- self_out: bfloat16 [768, 768], P('mp'), may hold values from -2 to 2
- cross_gain: float32 [768], replicated, may hold values from 0.5 to 1.5
- cross_query: bfloat16 [768, 768], P(None, 'mp'), may hold values from -0.21875 to 0.21875
- cross_out: bfloat16 [768, 768], P('mp'), may hold values from -6 to 6
- ffn_gain: float32 [768], replicated, may hold values from 0.5 to 1.5
- ffn_in: bfloat16 [768, 3072], P(None, 'mp'), may hold values from -0.21875 to 0.21875
- ffn_out: bfloat16 [3072, 768], P('mp'), may hold values from -0.109375 to 0.109375
Outputs:
- layer_out: bfloat16 [16, 512, 768], P('dp')
- input_grad: float32 [16, 512, 768], P('dp')
- memory_grad: float32 [16, 2, 16, 128, 768], P('dp', 'mp')
- group_gain_grad: float32 [768], P('dp')
- group_bias_grad: float32 [768], P('dp')
- conv_grad: float32 [768, 768], P('dp')
- cross_kv_grad: float32 [768, 2, 768], P('dp')
- self_gain_grad: float32 [768], P('dp')
- self_qkv_grad: float32 [768, 3, 768], P('dp', None, 'mp')
- self_out_grad: float32 [768, 768], P('mp', 'dp')
- cross_gain_grad: float32 [768], P('dp')
- cross_query_grad: float32 [768, 768], P('dp', 'mp')
- cross_out_grad: float32 [768, 768], P('mp', 'dp')
- ffn_gain_grad: float32 [768], P('dp')
- ffn_in_grad: float32 [768, 3072], P('dp', 'mp')
- ffn_out_grad: float32 [3072, 768], P('mp', 'dp')
Inputs may be any that keep to these rules, and one draw needn't show every extreme that they name: `mem_lengths`: one document, drawn from the seed, has exactly 4096 memory tokens. `dec_lengths`: one slot, drawn from the seed, has exactly 512 decoder tokens. `doc_owner`: each document is read by exactly one decoder slot.
All inputs are finite; a program needn't handle non-finite values.
Results may differ from a plain program's by a relative error of at most 0.015.
Values may be sent and summed in bfloat16 or wider, within the bound.
No kernel may reach another device: no remote copies, remote signals or barrier semaphores. Data moves between devices by JAX's collectives and lax.ppermute only.
A program may use at most 256 MiB of HBM per device.

v0:
```python
from functools import partial

import jax
import jax.numpy as jnp
from jax import lax
from jax.sharding import PartitionSpec as P

HD = 64
GROUPS = 32
DEC = 512


norm_eps = 1e-06
group_eps = 1e-05
masked_fill = -1000000000.0


def round_low(values):
    return lax.optimization_barrier(values.astype(jnp.bfloat16)).astype(jnp.float32)


def norm_rows(values, gain):
    factor = lax.rsqrt(jnp.mean(values * values, axis=-1, keepdims=True) + norm_eps)
    return (values * factor * gain, factor)


def norm_rows_back(values, factor, gain, incoming):
    scaled = incoming * gain
    inward = factor * scaled - values * factor * factor * factor * jnp.mean(
        scaled * values, axis=-1, keepdims=True
    )
    gain_grad = jnp.sum(incoming * values * factor, axis=0)
    return (inward, gain_grad)


def head_total(partial_sum):
    return lax.psum(partial_sum, "mp")


def attend(queries, key_rows, values, allowed):
    scores = (
        jnp.einsum("hne,hme->hnm", queries, key_rows, preferred_element_type=jnp.float32) * 0.125
    )
    scores = jnp.where(allowed, scores, masked_fill)
    row_max = jnp.max(scores, axis=-1, keepdims=True)
    shifted = jnp.exp(scores - row_max)
    row_total = jnp.sum(shifted, axis=-1, keepdims=True)
    weights = (shifted / row_total).astype(jnp.bfloat16)
    output = jnp.einsum("hnm,hme->hne", weights, values, preferred_element_type=jnp.float32)
    return (output.astype(jnp.bfloat16), (row_max + jnp.log(row_total))[..., 0])


def attend_back(queries, key_rows, values, allowed, log_total, grad_output):
    scores = (
        jnp.einsum("hne,hme->hnm", queries, key_rows, preferred_element_type=jnp.float32) * 0.125
    )
    scores = jnp.where(allowed, scores, masked_fill)
    probs = jnp.exp(scores - log_total[..., None])
    grad_probs = jnp.einsum("hne,hme->hnm", grad_output, values, preferred_element_type=jnp.float32)
    grad_scores = probs * (grad_probs - jnp.sum(probs * grad_probs, axis=-1, keepdims=True))
    grad_low = grad_scores.astype(jnp.bfloat16)
    query_grad = (
        jnp.einsum("hnm,hme->hne", grad_low, key_rows, preferred_element_type=jnp.float32) * 0.125
    )
    key_grad = (
        jnp.einsum("hnm,hne->hme", grad_low, queries, preferred_element_type=jnp.float32) * 0.125
    )
    value_grad = jnp.einsum(
        "hnm,hne->hme", probs.astype(jnp.bfloat16), grad_output, preferred_element_type=jnp.float32
    )
    return (query_grad, key_grad, value_grad)


def shards(
    dec_input,
    out_grad,
    enc_feats,
    mem_lengths,
    dec_lengths,
    doc_owner,
    group_gain,
    group_bias,
    conv_weight,
    cross_kv,
    self_gain,
    self_qkv,
    self_out,
    cross_gain,
    cross_query,
    cross_out,
    ffn_gain,
    ffn_in,
    ffn_out,
):
    chip_count = lax.axis_size("dp")
    core_count = lax.axis_size("mp")
    chip_index = lax.axis_index("dp")
    core_index = lax.axis_index("mp")
    memory_in = enc_feats[0, 0]
    doc_count, sub_rows, model_width = memory_in.shape
    per_group = model_width // GROUPS
    half_width = model_width // core_count
    heads_here = half_width // HD
    own_docs = dec_input.shape[0]
    dec_rows = own_docs * DEC
    mem_rows = doc_count * sub_rows
    slot_pos = lax.broadcasted_iota(jnp.int32, (doc_count, sub_rows), 1)
    position = (slot_pos * core_count + core_index) * chip_count + chip_index
    live_mask = (position < mem_lengths[:, None]).astype(jnp.float32)
    live_groups = live_mask[:, :, None, None]
    memory_wide = memory_in.astype(jnp.float32)
    grouped = memory_wide.reshape(doc_count, sub_rows, GROUPS, per_group)
    masked = grouped * live_groups
    first_sum = jnp.sum(masked, axis=(1, 3))
    second_sum = jnp.sum(masked * grouped, axis=(1, 3))
    first_sum, second_sum = lax.psum((first_sum, second_sum), ("dp", "mp"))
    entries = (mem_lengths * per_group).astype(jnp.float32)[:, None]
    center = first_sum / entries
    spread = lax.rsqrt(second_sum / entries - center * center + group_eps)
    normed_groups = (grouped - center[:, None, :, None]) * spread[:, None, :, None]
    normed = normed_groups.reshape(doc_count, sub_rows, model_width)
    activation_in = normed * group_gain + group_bias
    silu_value, silu_back = jax.vjp(jax.nn.silu, activation_in)
    hidden_flat = silu_value.astype(jnp.bfloat16).reshape(mem_rows, model_width)
    memory = memory_wide.reshape(mem_rows, model_width) + jnp.dot(
        hidden_flat, conv_weight, preferred_element_type=jnp.float32
    )
    memory_low = memory.astype(jnp.bfloat16)
    pair_weight = (
        cross_kv.reshape(model_width, 2, core_count, half_width)
        .transpose(0, 2, 1, 3)
        .reshape(model_width, 2 * model_width)
    )
    pair_rows = jnp.dot(memory_low, pair_weight, preferred_element_type=jnp.float32).astype(
        jnp.bfloat16
    )
    pair_rows = pair_rows.reshape(doc_count, sub_rows, core_count, 2 * half_width)
    outgoing = jnp.take(pair_rows, doc_owner, axis=0).reshape(
        chip_count, own_docs, sub_rows, core_count, 2 * half_width
    )
    incoming = lax.all_to_all(
        lax.all_to_all(outgoing, "dp", split_axis=0, concat_axis=0, tiled=True),
        "mp",
        split_axis=3,
        concat_axis=2,
        tiled=True,
    )
    input_flat = dec_input.astype(jnp.float32).reshape(dec_rows, model_width)
    normed_one, factor_one = norm_rows(input_flat, self_gain)
    normed_one = normed_one.astype(jnp.bfloat16)
    qkv_self = jnp.einsum(
        "td,dkf->tkf", normed_one, self_qkv, preferred_element_type=jnp.float32
    ).astype(jnp.bfloat16)
    qkv_heads = qkv_self.reshape(own_docs, DEC, 3, heads_here, HD).transpose(0, 2, 3, 1, 4)
    row_pos = lax.broadcasted_iota(jnp.int32, (DEC, DEC), 0)
    col_pos = lax.broadcasted_iota(jnp.int32, (DEC, DEC), 1)
    slot_base = chip_index * own_docs
    local = 0
    allowed = (col_pos <= row_pos) & (col_pos < dec_lengths[slot_base + local])
    output, log_total = attend(
        qkv_heads[local, 0], qkv_heads[local, 1], qkv_heads[local, 2], allowed[None]
    )
    self_masks = [allowed]
    self_outputs = [output]
    self_totals = [log_total]
    attended = jnp.stack(self_outputs).transpose(0, 2, 1, 3).reshape(dec_rows, half_width)
    first_out = input_flat + head_total(
        jnp.dot(attended, self_out, preferred_element_type=jnp.float32)
    )
    normed_two, factor_two = norm_rows(first_out, cross_gain)
    normed_two = normed_two.astype(jnp.bfloat16)
    cross_rows = jnp.dot(normed_two, cross_query, preferred_element_type=jnp.float32).astype(
        jnp.bfloat16
    )
    cross_heads = cross_rows.reshape(own_docs, DEC, heads_here, HD).transpose(0, 2, 1, 3)
    chip_pos = lax.broadcasted_iota(jnp.int32, (chip_count, core_count, sub_rows), 0)
    core_pos = lax.broadcasted_iota(jnp.int32, (chip_count, core_count, sub_rows), 1)
    sub_pos = lax.broadcasted_iota(jnp.int32, (chip_count, core_count, sub_rows), 2)
    key_position = ((sub_pos * core_count + core_pos) * chip_count + chip_pos).reshape(-1)
    mem_keys = key_position.shape[0]
    local = 0
    document = doc_owner[slot_base + local]
    key_live = key_position < mem_lengths[document]
    doc_pairs = (
        incoming[:, local, :, 0, :].reshape(mem_keys, 2, heads_here, HD).transpose(1, 2, 0, 3)
    )

    def one_head(items, key_live=key_live):
        query_head, key_head, value_head = items
        output, log_total = attend(
            query_head[None], key_head[None], value_head[None], key_live[None, None, :]
        )
        return (output[0], log_total[0])

    output, log_total = lax.map(one_head, (cross_heads[local], doc_pairs[0], doc_pairs[1]))
    cross_live = [key_live]
    cross_pairs = [doc_pairs]
    cross_outputs = [output]
    cross_totals = [log_total]
    crossed = jnp.stack(cross_outputs).transpose(0, 2, 1, 3).reshape(dec_rows, half_width)
    second_out = first_out + head_total(
        jnp.dot(crossed, cross_out, preferred_element_type=jnp.float32)
    )
    normed_three, factor_three = norm_rows(second_out, ffn_gain)
    normed_three = normed_three.astype(jnp.bfloat16)
    lifted = jnp.dot(normed_three, ffn_in, preferred_element_type=jnp.float32)
    gelu_value, gelu_back = jax.vjp(partial(jax.nn.gelu, approximate=True), lifted)
    active_low = gelu_value.astype(jnp.bfloat16)
    result = second_out + head_total(
        jnp.dot(active_low, ffn_out, preferred_element_type=jnp.float32)
    )
    layer_out = result.astype(jnp.bfloat16).reshape(own_docs, DEC, model_width)
    grad_low = out_grad.reshape(dec_rows, model_width)
    grad_result = grad_low.astype(jnp.float32)
    ffn_out_grad = jnp.dot(active_low.T, grad_low, preferred_element_type=jnp.float32)
    grad_active = jnp.dot(grad_low, ffn_out.T, preferred_element_type=jnp.float32).astype(
        jnp.bfloat16
    )
    grad_lifted = gelu_back(grad_active.astype(jnp.float32))[0].astype(jnp.bfloat16)
    ffn_in_grad = jnp.dot(normed_three.T, grad_lifted, preferred_element_type=jnp.float32)
    grad_normed_three = round_low(
        head_total(jnp.dot(grad_lifted, ffn_in.T, preferred_element_type=jnp.float32))
    )
    grad_second, ffn_gain_grad = norm_rows_back(
        second_out, factor_three, ffn_gain, grad_normed_three
    )
    grad_second = grad_second + grad_result
    grad_cross = grad_second.astype(jnp.bfloat16)
    cross_out_grad = jnp.dot(crossed.T, grad_cross, preferred_element_type=jnp.float32)
    grad_crossed = jnp.dot(grad_cross, cross_out.T, preferred_element_type=jnp.float32).astype(
        jnp.bfloat16
    )
    grad_crossed = grad_crossed.reshape(own_docs, DEC, heads_here, HD).transpose(0, 2, 1, 3)
    local = 0
    key_live = cross_live[local]
    doc_pairs = cross_pairs[local]

    def one_head_back(items, key_live=key_live):
        query_head, key_head, value_head, total_head, grad_head = items
        query_grad, key_grad, value_grad = attend_back(
            query_head[None],
            key_head[None],
            value_head[None],
            key_live[None, None, :],
            total_head[None],
            grad_head[None],
        )
        return (query_grad[0], key_grad[0], value_grad[0])

    query_grad, key_grad, value_grad = lax.map(
        one_head_back,
        (cross_heads[local], doc_pairs[0], doc_pairs[1], cross_totals[local], grad_crossed[local]),
    )
    query_grads = [query_grad]
    both_grads = jnp.stack((key_grad, value_grad)).transpose(2, 0, 1, 3)
    pair_grads = [both_grads.reshape(chip_count, core_count * sub_rows, 2 * half_width)]
    owned_grads = jnp.stack(pair_grads, axis=1).astype(jnp.bfloat16)
    inverse = (
        jnp.zeros((doc_count,), jnp.int32).at[doc_owner].set(jnp.arange(doc_count, dtype=jnp.int32))
    )
    returning = owned_grads[:, :, :, None, :]
    returned = lax.all_to_all(
        lax.all_to_all(returning, "dp", split_axis=0, concat_axis=0, tiled=True),
        "mp",
        split_axis=2,
        concat_axis=3,
        tiled=True,
    )
    returned = returned.reshape(doc_count, sub_rows, 2 * model_width)
    pair_grad_rows = jnp.take(returned, inverse, axis=0).reshape(mem_rows, 2 * model_width)
    pair_weight_grad = jnp.dot(memory_low.T, pair_grad_rows, preferred_element_type=jnp.float32)
    cross_kv_part = (
        pair_weight_grad.reshape(model_width, core_count, 2, half_width)
        .transpose(0, 2, 1, 3)
        .reshape(model_width, 2, model_width)
    )
    grad_memory_low = jnp.dot(
        pair_grad_rows, pair_weight.T, preferred_element_type=jnp.float32
    ).astype(jnp.bfloat16)
    grad_query_rows = (
        jnp.stack(query_grads)
        .transpose(0, 2, 1, 3)
        .reshape(dec_rows, half_width)
        .astype(jnp.bfloat16)
    )
    cross_query_grad = jnp.dot(normed_two.T, grad_query_rows, preferred_element_type=jnp.float32)
    grad_normed_two = round_low(
        head_total(jnp.dot(grad_query_rows, cross_query.T, preferred_element_type=jnp.float32))
    )
    grad_first, cross_gain_grad = norm_rows_back(first_out, factor_two, cross_gain, grad_normed_two)
    grad_first = grad_first + grad_second
    grad_self = grad_first.astype(jnp.bfloat16)
    self_out_grad = jnp.dot(attended.T, grad_self, preferred_element_type=jnp.float32)
    grad_attended = jnp.dot(grad_self, self_out.T, preferred_element_type=jnp.float32).astype(
        jnp.bfloat16
    )
    grad_attended = grad_attended.reshape(own_docs, DEC, heads_here, HD).transpose(0, 2, 1, 3)
    local = 0
    query_grad, key_grad, value_grad = attend_back(
        qkv_heads[local, 0],
        qkv_heads[local, 1],
        qkv_heads[local, 2],
        self_masks[local][None],
        self_totals[local],
        grad_attended[local],
    )
    triple_grads = [jnp.stack((query_grad, key_grad, value_grad))]
    grad_qkv = (
        jnp.stack(triple_grads)
        .transpose(0, 3, 1, 2, 4)
        .reshape(dec_rows, 3, half_width)
        .astype(jnp.bfloat16)
    )
    self_qkv_grad = jnp.einsum(
        "td,tkf->dkf", normed_one, grad_qkv, preferred_element_type=jnp.float32
    )
    grad_normed_one = round_low(
        head_total(
            jnp.einsum("tkf,dkf->td", grad_qkv, self_qkv, preferred_element_type=jnp.float32)
        )
    )
    grad_input, self_gain_grad = norm_rows_back(input_flat, factor_one, self_gain, grad_normed_one)
    input_grad = (grad_input + grad_first).reshape(own_docs, DEC, model_width)
    conv_part = jnp.dot(hidden_flat.T, grad_memory_low, preferred_element_type=jnp.float32)
    grad_hidden = jnp.dot(
        grad_memory_low, conv_weight.T, preferred_element_type=jnp.float32
    ).reshape(doc_count, sub_rows, model_width)
    grad_act = silu_back(grad_hidden)[0]
    gain_part = jnp.sum(grad_act * normed, axis=(0, 1))
    bias_part = jnp.sum(grad_act, axis=(0, 1))
    grad_normed = (grad_act * group_gain).reshape(doc_count, sub_rows, GROUPS, per_group)
    first_back = jnp.sum(grad_normed * live_groups, axis=(1, 3))
    second_back = jnp.sum(grad_normed * normed_groups * live_groups, axis=(1, 3))
    first_back, second_back = lax.psum((first_back, second_back), ("dp", "mp"))
    grad_wide = (
        spread[:, None, :, None]
        * (
            grad_normed
            - (first_back / entries)[:, None, :, None]
            - normed_groups * (second_back / entries)[:, None, :, None]
        )
        * live_groups
    )
    memory_grad = grad_memory_low.astype(jnp.float32) + grad_wide.reshape(mem_rows, model_width)
    memory_grad = memory_grad.reshape(1, 1, doc_count, sub_rows, model_width)
    conv_part, cross_kv_part, gain_part, bias_part = (
        lax.psum(conv_part.astype(jnp.bfloat16), "mp").astype(jnp.float32),
        lax.psum(cross_kv_part.astype(jnp.bfloat16), "mp").astype(jnp.float32),
        lax.psum(gain_part.astype(jnp.bfloat16), "mp").astype(jnp.float32),
        lax.psum(bias_part.astype(jnp.bfloat16), "mp").astype(jnp.float32),
    )
    row_sums = (
        lax.psum_scatter(self_qkv_grad, "dp", scatter_dimension=0, tiled=True),
        lax.psum_scatter(cross_query_grad, "dp", scatter_dimension=0, tiled=True),
        lax.psum_scatter(ffn_in_grad, "dp", scatter_dimension=0, tiled=True),
        lax.psum_scatter(self_gain_grad, "dp", scatter_dimension=0, tiled=True),
        lax.psum_scatter(cross_gain_grad, "dp", scatter_dimension=0, tiled=True),
        lax.psum_scatter(ffn_gain_grad, "dp", scatter_dimension=0, tiled=True),
        lax.psum_scatter(conv_part, "dp", scatter_dimension=0, tiled=True),
        lax.psum_scatter(cross_kv_part, "dp", scatter_dimension=0, tiled=True),
        lax.psum_scatter(gain_part, "dp", scatter_dimension=0, tiled=True),
        lax.psum_scatter(bias_part, "dp", scatter_dimension=0, tiled=True),
    )
    column_sums = (
        lax.psum_scatter(self_out_grad, "dp", scatter_dimension=1, tiled=True),
        lax.psum_scatter(cross_out_grad, "dp", scatter_dimension=1, tiled=True),
        lax.psum_scatter(ffn_out_grad, "dp", scatter_dimension=1, tiled=True),
    )
    conv_grad, cross_kv_grad, group_gain_grad, group_bias_grad = (
        row_sums[6],
        row_sums[7],
        row_sums[8],
        row_sums[9],
    )
    return (
        layer_out,
        input_grad,
        memory_grad,
        group_gain_grad,
        group_bias_grad,
        conv_grad,
        cross_kv_grad,
        row_sums[3],
        row_sums[0],
        column_sums[0],
        row_sums[4],
        row_sums[1],
        column_sums[1],
        row_sums[5],
        row_sums[2],
        column_sums[2],
    )


def solution(mesh):
    placed = (
        P("dp", None, None),
        P("dp", None, None),
        P("dp", "mp", None, None, None),
        P(),
        P(),
        P(),
        P(),
        P(),
        P(),
        P(),
        P(),
        P(None, None, "mp"),
        P("mp", None),
        P(),
        P(None, "mp"),
        P("mp", None),
        P(),
        P(None, "mp"),
        P("mp", None),
    )
    return jax.shard_map(
        shards,
        mesh=mesh,
        in_specs=placed,
        out_specs=(
            P("dp", None, None),
            P("dp", None, None),
            P("dp", "mp", None, None, None),
            P("dp"),
            P("dp"),
            P("dp", None),
            P("dp", None, None),
            P("dp"),
            P("dp", None, "mp"),
            P("mp", "dp"),
            P("dp"),
            P("dp", "mp"),
            P("mp", "dp"),
            P("dp"),
            P("dp", "mp"),
            P("mp", "dp"),
        ),
        check_vma=False,
    )
```

profile of v0, /device:TPU:0, one launch (start us, length us, event | category | flops | bytes accessed | tf_op | source)
XLA Modules:
  0.0 2076.7 jit_solution(7790416205264309384)
XLA Ops:
  26.0 42.6 %all-reduce.7 = (f32[16,32]{1,0:T(8,128)S(1)}, f32[16,32]{1,0:T(8,128)S(1)}) all-reduce(f32[16,32]{1,0:T(8,128)S(1)} %reduce_sum.193, f32[16,32]{1,0:T(8,128)S(1)} %reduce_sum.190), channel_id=1, replica_groups=mesh['dp'=16,'mp'=2] {'dp','mp'}, use_global_device_ids=true, to_apply=%region_10.11 | all-reduce | flops 1024 | bytes 8192 | tf_op jit(solution)/shard_map/psum | solution.py:116
  69.9 6.7 copy.190
  88.6 7.1 convolution_convert_fusion
  95.6 13.6 reshape.453
  109.2 6.8 copy.192
  116.0 6.4 gather_fusion
  122.4 6.2 fusion.61
  149.7 18.6 all-reduce.20.cloned.1.call-done
  173.9 76.5 %all-to-all-done = bf16[16,1,128,2,768]{4,2,3,1,0:T(8,128)(2,1)} async-done(((bf16[16,1,128,2,768]{4,2,3,1,0:T(8,128)(2,1)}), bf16[16,1,128,2,768]{4,2,3,1,0:T(8,128)(2,1)}, u32[]{:S(2)}, u32[]{:S(2)}) %all-to-all-start) | async-done | bytes 6291488 | tf_op jit(solution)/shard_map/all_to_all | solution.py:142
  253.6 10.2 all_to_all.40
  263.7 16.3 copy.195
  280.0 11.1 reshape_squeeze.3
  291.2 6.3 slice_bitcast_fusion
  297.4 6.5 copy.196
  304.0 6.5 copy.197
  310.5 83.5 %while.28 = (s32[]{:T(128)}, bf16[6,512,64]{1,2,0:T(8,128)(2,1)S(1)}, f32[6,512]{1,0:T(8,128)}, bf16[6,512,64]{2,1,0:T(8,128)(2,1)S(1)}, bf16[6,4096,64]{2,1,0:T...) while((s32[]{:T(128)}, ...), condition=%wide.region_14.15_spmd.clone, body=%wide.region_11.14_spmd.clone.sunk | while | flops 562085376 | bytes 61065920 | solution.py:195
  397.3 43.2 %all-reduce.22.cloned.1.call-done = f32[512,768]{1,0:T(8,128)} async-done(((f32[512,768]{1,0:T(8,128)}), f32[512,768]{1,0:T(8,128)}) %all-reduce.22.cloned.1.call-update) | async-done | bytes 1572880 | tf_op jit(solution)/shard_map/psum | solution.py:37
  458.0 8.8 all-reduce.29
  467.9 11.8 all-reduce.24.cloned.1.call-done
  485.0 178.4 %while.29 = (s32[]{:T(128)}, bf16[6,512,64]{1,2,0:T(8,128)(2,1)S(1)}, bf16[6,4096,64]{1,2,0:T(8,128)(2,1)}, bf16[6,4096,64]{1,2,0:T(8,128)(2,1)}, bf16[6,512,64]...) while((s32[]{:T(128)}, ...), condition=%wide.region_22.23_spmd.clone, body=%wide.region_20.22_spmd.clone.sunk | while | flops 1361362432 | bytes 105545424 | solution.py:250
  485.1 6.0 fusion.227
  492.5 7.1 multiply_reduce_fusion.9
  499.6 7.9 multiply_convert_fusion.14
  522.1 7.1 multiply_reduce_fusion.9
  529.3 7.9 multiply_convert_fusion.14
  551.8 7.1 multiply_reduce_fusion.9
  559.0 7.9 multiply_convert_fusion.14
  581.4 7.1 multiply_reduce_fusion.9
  588.6 7.9 multiply_convert_fusion.14
  611.1 7.1 multiply_reduce_fusion.9
  618.2 7.9 multiply_convert_fusion.14
  640.7 7.1 multiply_reduce_fusion.9
  647.9 7.9 multiply_convert_fusion.14
  674.3 6.9 all-to-all-start.2
  682.1 119.1 %all-to-all-done.2 = bf16[16,1,256,1,768]{2,4,3,1,0:T(8,128)(2,1)} async-done(((bf16[16,1,256,1,768]{2,4,3,1,0:T(8,128)(2,1)}), bf16[16,1,256,1,768]{2,4,3,1,0:T(8,128)(2,1)}, u32[]{:S(2)}, u32[]{:S(2)}) %all-to-all-start.2) | async-done | bytes 6291488 | tf_op jit(solution)/shard_map/all_to_all | solution.py:263
  801.2 8.9 copy.206
  810.1 10.4 all_to_all.41
  825.4 8.6 copy.208
  834.0 8.6 copy.209
  842.6 6.4 gather_fusion.1
  849.0 6.3 broadcast_select_fusion
  859.1 8.7 copy.223
  867.7 8.1 convert_bitcast_fusion.2
  878.4 8.4 convolution_convert_fusion.1
  890.5 47.8 %all-reduce.28.cloned.1.call-done = (bf16[768,2,768]{0,2,1:T(8,128)(2,1)}, bf16[768,768]{1,0:T(8,128)(2,1)}) async-done(((bf16[768,2,768]{0,2,1:T(8,128)(2,1)}, bf16[768,768]{1,0:T(8,128)(2,1)}), (bf16[768,2,768]{0,2,1:T(8,128)(2,1)}, bf16[768,768]{1,0:T(8,128)(2,1)})) %all-reduce.28.cloned.1.call-update) | async-done | bytes 3538960 | tf_op jit(solution)/shard_map/psum | solution.py:348
  938.3 7.2 copy.225
  953.3 8.4 all-reduce.30
  1007.5 6.7 copy.212
  1020.4 6.7 copy.222
  1034.6 8.7 all-reduce.31
  1050.4 6.5 copy.214
  1062.0 7.7 multiply_reduce_fusion.3
  1069.8 42.5 %all-reduce.6 = (f32[16,32]{1,0:T(8,128)S(1)}, f32[16,32]{1,0:T(8,128)S(1)}) all-reduce(f32[16,32]{1,0:T(8,128)S(1)} %copy.216, f32[16,32]{1,0:T(8,128)S(1)} %copy.219), channel_id=1, replica_groups=mesh['dp'=16,'mp'=2] {'dp','mp'}, use_global_device_ids=true, to_apply=%region_30.31 | all-reduce | flops 1024 | bytes 8192 | tf_op jit(solution)/shard_map/psum | solution.py:334
  1118.6 6.6 copy.218
  1131.5 6.6 copy.221
  1138.1 17.4 fusion.60
  1162.2 75.7 %all-reduce.8 = (f32[768]{0:T(1024)S(1)}, f32[768]{0:T(1024)S(1)}, f32[768]{0:T(1024)S(1)}, f32[768]{0:T(1024)S(1)}, f32[768]{0:T(1024)S(1)}) all-reduce(bf16[768]{0:T(1024)(128)(2,1)S(1)} %get-tuple-element.361, bf16[768]{0:T(1024)(128)(2,1)S(1)} %get-tuple-element.362, ...), channel_id=2, replica_groups=mesh['dp'=16,'mp'=2] {'dp'}, use_global_device_ids=true, to_apply=%region_35.36.clone | all-reduce | flops 3840 | bytes 27648
  1242.6 13.5 reduce-scatter.16.cloned.1.call-done
  1256.0 128.7 %reduce-scatter.14.cloned.1.call-done = f32[48,384]{1,0:T(8,128)} async-done(((f32[768,384]{1,0:T(8,128)}), f32[48,384]{1,0:T(8,128)}) %reduce-scatter.14.cloned.1.call-update) | async-done | bytes 73744 | tf_op jit(solution)/shard_map/reduce_scatter | solution.py:354
  1384.7 128.5 %reduce-scatter.12.cloned.1.call-done = f32[384,48]{0,1:T(8,128)} async-done(((f32[384,768]{0,1:T(8,128)}), f32[384,48]{0,1:T(8,128)}) %reduce-scatter.12.cloned.1.call-update) | async-done | bytes 73744 | tf_op jit(solution)/shard_map/reduce_scatter | solution.py:365
  1513.2 139.2 %reduce-scatter.10.cloned.1.call-done = f32[48,3,384]{2,0,1:T(8,128)} async-done(((f32[768,3,384]{2,0,1:T(8,128)}), f32[48,3,384]{2,0,1:T(8,128)}) %reduce-scatter.10.cloned.1.call-update) | async-done | bytes 221200 | tf_op jit(solution)/shard_map/reduce_scatter | solution.py:353
  1652.4 142.5 %reduce-scatter.18.cloned.1.call-done = f32[48,1536]{1,0:T(8,128)} async-done(((f32[768,1536]{1,0:T(8,128)}), f32[48,1536]{1,0:T(8,128)}) %reduce-scatter.18.cloned.1.call-update) | async-done | bytes 294928 | tf_op jit(solution)/shard_map/reduce_scatter | solution.py:355
  1795.0 141.9 %reduce-scatter.20.cloned.1.call-done = f32[1536,48]{0,1:T(8,128)} async-done(((f32[1536,768]{0,1:T(8,128)}), f32[1536,48]{0,1:T(8,128)}) %reduce-scatter.20.cloned.1.call-update) | async-done | bytes 294928 | tf_op jit(solution)/shard_map/reduce_scatter | solution.py:367
  1936.9 132.8 %reduce-scatter.8.cloned.1.call-done = f32[48,768]{1,0:T(8,128)} async-done(((f32[768,768]{1,0:T(8,128)}), f32[48,768]{1,0:T(8,128)}) %reduce-scatter.8.cloned.1.call-update) | async-done | bytes 147472 | tf_op jit(solution)/shard_map/reduce_scatter | solution.py:359
  (507 shorter events, 379.6 us)
Async XLA Ops:
  7.2 439.2 %copy-start = (bf16[1536,768]{1,0:T(8,128)(2,1)S(1)}, bf16[1536,768]{1,0:T(8,128)(2,1)}, u32[]{:S(2)}) copy-start(bf16[1536,768]{1,0:T(8,128)(2,1)} %param.41) | copy-start | bytes 7077892
  8.0 108.0 %copy-start.90 = (s32[16]{0:T(128)}, s32[16]{0:T(128)S(1)}, u32[]{:S(2)}) copy-start(s32[16]{0:T(128)S(1)} %compare_select_fusion.1) | copy-start | bytes 196
  9.3 59.3 %copy-start.84 = (f32[16]{0:T(128)}, f32[16]{0:T(128)S(1)}, u32[]{:S(2)}) copy-start(f32[16]{0:T(128)S(1)} %multiply_convert_fusion.6) | copy-start | bytes 196
  10.1 10.0 copy-start.53
  69.6 9.0 copy-start.39
  69.9 8.7 copy-start.41
  76.7 6.9 slice-start.2
  78.7 8.3 copy-start.25
  128.6 5.9 copy-start.95
  128.6 7.1 copy-start.14
  128.6 7.5 copy-start.69
  128.6 121.8 %all-to-all-start = ((bf16[16,1,128,2,768]{4,2,3,1,0:T(8,128)(2,1)}), bf16[16,1,128,2,768]{4,2,3,1,0:T(8,128)(2,1)}, u32[]{:S(2)}, u32[]{:S(2)}) async-start(bf16[16,1,128,2,768]{4,2,3,1,0:T(8,128)(2,1)} %fusion.61), calls=%async_computation | async-start | bytes 12582912 | tf_op jit(solution)/shard_map/all_to_all | solution.py:142
  134.2 34.0 %all-reduce.20.cloned.1.call-start = ((), (), s32[]{:S(2)}) async-start(), calls=%async_computation.11 | async-start | bytes 3145728 | tf_op jit(solution)/shard_map/psum | solution.py:37
  146.4 24.7 %copy-start.61 = (f32[768]{0:T(1024)S(1)}, f32[768]{0:T(1024)}, u32[]{:S(2)}) copy-start(f32[768]{0:T(1024)} %param.36) | copy-start | bytes 9220
  146.5 294.1 %all-reduce.22.cloned.1.call-start = ((), (), s32[]{:S(2)}) async-start(), calls=%async_computation.12 | async-start | bytes 3145728 | tf_op jit(solution)/shard_map/psum | solution.py:37
  170.0 83.5 %copy-start.67 = (f32[512]{0:T(512)}, f32[512]{0:T(512)S(1)}, u32[]{:S(2)}) copy-start(f32[512]{0:T(512)S(1)} %add_rsqrt_fusion.2) | copy-start | bytes 6148
  332.5 5.8 copy-start.66
  346.4 5.9 copy-start.66
  374.2 5.9 copy-start.66
  388.1 5.9 copy-start.66
  394.0 48.8 %copy-start.32 = (bf16[6,512,64]{1,2,0:T(8,128)(2,1)}, bf16[6,512,64]{1,2,0:T(8,128)(2,1)S(1)}, u32[]{:S(2)}) copy-start(bf16[6,512,64]{1,2,0:T(8,128)(2,1)S(1)} %get-tuple-element.108) | copy-start | bytes 1179652
  396.9 45.9 %copy-start.45 = (f32[768]{0:T(1024)S(1)}, f32[768]{0:T(1024)}, u32[]{:S(2)}) copy-start(f32[768]{0:T(1024)} %param.39) | copy-start | bytes 9220
  397.0 82.8 %all-reduce.24.cloned.1.call-start = ((), (), s32[]{:S(2)}) async-start(), calls=%async_computation.13 | async-start | bytes 3145728 | tf_op jit(solution)/shard_map/psum | solution.py:37
  442.8 36.9 %copy-start.63 = (f32[512]{0:T(512)}, f32[512]{0:T(512)S(1)}, u32[]{:S(2)}) copy-start(f32[512]{0:T(512)S(1)} %add_rsqrt_fusion.1) | copy-start | bytes 6148
  449.5 5.9 copy-start.92
  458.0 8.8 copy-start.9
  485.0 7.4 copy-start.16
  514.7 7.4 copy-start.16
  544.4 7.4 copy-start.16
  574.0 7.4 copy-start.16
  603.6 7.4 copy-start.16
  633.3 7.4 copy-start.16
  674.3 126.9 %all-to-all-start.2 = ((bf16[16,1,256,1,768]{2,4,3,1,0:T(8,128)(2,1)}), bf16[16,1,256,1,768]{2,4,3,1,0:T(8,128)(2,1)}, u32[]{:S(2)}, u32[]{:S(2)}) async-start(bf16[16,1,256,1,768]{2,4,3,1,0:T(8,128)(2,1)} %copy.205), calls=%async_computation.2 | async-start | bytes 12582912 | tf_op jit(solution)/shard_map/all_to_all | solution.py:263
  681.1 257.1 %all-reduce.28.cloned.1.call-start = ((), (), s32[]{:S(2)}) async-start(), calls=%async_computation.22 | async-start | bytes 7077888 | tf_op jit(solution)/shard_map/psum | solution.py:348
  849.0 6.3 copy-start.5
  878.4 8.4 copy-start.19
  890.5 350.4 %all-reduce.26.cloned.1.call-start = ((), (), s32[]{:S(2)}) async-start(), calls=%async_computation.21 | async-start | bytes 9437184
  945.5 5.9 copy-start.7
  945.5 5.9 copy-start.62
  945.6 5.9 copy-start.68
  945.6 310.5 %reduce-scatter.16.cloned.1.call-start = ((), (), s32[]{:S(2)}) async-start(), calls=%async_computation.18 | async-start | bytes 1253376 | tf_op jit(solution)/shard_map/reduce_scatter | solution.py:366
  949.5 435.1 %reduce-scatter.14.cloned.1.call-start = ((), (), s32[]{:S(2)}) async-start(), calls=%async_computation.17 | async-start | bytes 1253376 | tf_op jit(solution)/shard_map/reduce_scatter | solution.py:354
  953.2 560.0 %reduce-scatter.12.cloned.1.call-start = ((), (), s32[]{:S(2)}) async-start(), calls=%async_computation.16 | async-start | bytes 1253376 | tf_op jit(solution)/shard_map/reduce_scatter | solution.py:365
  967.6 684.8 %reduce-scatter.10.cloned.1.call-start = ((), (), s32[]{:S(2)}) async-start(), calls=%async_computation.15 | async-start | bytes 3760128 | tf_op jit(solution)/shard_map/reduce_scatter | solution.py:353
  980.5 814.5 %reduce-scatter.18.cloned.1.call-start = ((), (), s32[]{:S(2)}) async-start(), calls=%async_computation.19 | async-start | bytes 5013504 | tf_op jit(solution)/shard_map/reduce_scatter | solution.py:355
  987.0 949.9 %reduce-scatter.20.cloned.1.call-start = ((), (), s32[]{:S(2)}) async-start(), calls=%async_computation.20 | async-start | bytes 5013504 | tf_op jit(solution)/shard_map/reduce_scatter | solution.py:367
  993.8 1075.9 %reduce-scatter.8.cloned.1.call-start = ((), (), s32[]{:S(2)}) async-start(), calls=%async_computation.14 | async-start | bytes 2506752 | tf_op jit(solution)/shard_map/reduce_scatter | solution.py:359
  994.6 6.7 copy-start.47
  994.6 6.0 copy-start.76
  1020.4 6.7 copy-start.97
  1020.4 7.9 copy-start.89
  1020.4 7.9 copy-start.87
  1034.6 8.7 copy-start.71
  1034.6 8.8 copy-start.80
  1034.6 9.5 copy-start.13
  1061.9 50.4 %copy-start.85 = (f32[16]{0:T(128)S(1)}, f32[16]{0:T(128)}, u32[]{:S(2)}) copy-start(f32[16]{0:T(128)} %copy-done.84) | copy-start | bytes 196
  1131.4 6.6 copy-start.40
  1131.4 6.6 copy-start.42
  1131.4 6.6 copy-start.74
  1131.4 6.7 copy-start.77
  1131.5 6.7 copy-start.81
  1155.5 6.7 copy-start.82
  1155.5 6.7 copy-start.83
  1155.5 914.2 %copy-start.1 = (bf16[1536,768]{1,0:T(8,128)(2,1)S(1)}, bf16[1536,768]{1,0:T(8,128)(2,1)}, u32[]{:S(2)}) copy-start(bf16[1536,768]{1,0:T(8,128)(2,1)} %param.41) | copy-start | bytes 7077892
  (86 other events, 262.4 us)
Sparse Core Ops, SparseCore 0:
  146.6 21.6 all-reduce.19
  397.1 43.3 all-reduce.21
  458.1 21.5 all-reduce.23
  890.6 47.6 all-reduce.27
  945.6 181.8 all-reduce.25
  1133.5 122.5 reduce-scatter.15
  1262.1 122.5 reduce-scatter.13
  1390.7 122.4 reduce-scatter.11
  1519.7 132.6 reduce-scatter.9
  1658.8 136.0 reduce-scatter.17
  1800.7 136.1 reduce-scatter.19
  1943.0 126.6 reduce-scatter.7
where the time goes:
time: 2090 us; the launch traced here: 2080 us
  waiting for transfers between devices  1140 us (55%)
  local copies, waits for them, and re-layouts  268 us (13%)
  matrix products  265 us (13%)
  blocking collectives  210 us (10%)
  other arithmetic  156 us (7%)
    reduce_scatter x1, waiting for transfers between devices, shards(): lax.psum_scatter(ffn_in_grad, 'dp', scatter_dimension=0, tiled=True)  143 us
    reduce_scatter x1, waiting for transfers between devices, shards(): lax.psum_scatter(ffn_out_grad, 'dp', scatter_dimension=1, tiled=True)  142 us
    reduce_scatter x1, waiting for transfers between devices, shards(): lax.psum_scatter(self_qkv_grad, 'dp', scatter_dimension=0, tiled=True)  139 us
    reduce_scatter x1, waiting for transfers between devices, shards(): lax.psum_scatter(conv_part, 'dp', scatter_dimension=0, tiled=True)  133 us
    reduce_scatter x1, waiting for transfers between devices, shards(): lax.psum_scatter(cross_query_grad, 'dp', scatter_dimension=0, tiled=True)  129 us
    reduce_scatter x1, waiting for transfers between devices, shards(): lax.psum_scatter(self_out_grad, 'dp', scatter_dimension=1, tiled=True)  129 us
    all_to_all x1, waiting for transfers between devices, shards(): lax.all_to_all(returning, 'dp', split_axis=0, concat_axis=0, tiled=True)  119 us
    all_to_all x1, waiting for transfers between devices, shards(): lax.all_to_all(outgoing, 'dp', split_axis=0, concat_axis=0, tiled=True)  76.5 us
  transfers between devices with their start and end apart: 14, of which 13 were waited for; matrix products, arithmetic and copies ran while one was open for 8% of the time, Pallas kernels for 0%

commit v1 on v0

v1 whole, which is shorter than its diff:
```python
from functools import partial

import jax
import jax.numpy as jnp
from jax import lax
from jax.experimental import pallas as pl
from jax.experimental.pallas import tpu as pltpu
from jax.sharding import PartitionSpec as P

HD = 64
GROUPS = 32
DEC = 512


norm_eps = 1e-06
group_eps = 1e-05
masked_fill = -1000000000.0
vmem_budget = 48 * 1024 * 1024
low_type = jnp.bfloat16
wide_type = jnp.float32


def dot_wide(left, right):
    return jnp.dot(left, right, preferred_element_type=wide_type)


def dot_rows(left, right):
    return lax.dot_general(left, right, (((0,), (0,)), ((), ())), preferred_element_type=wide_type)


def dot_columns(left, right):
    return lax.dot_general(left, right, (((1,), (1,)), ((), ())), preferred_element_type=wide_type)


def norm_rows(values, gain):
    factor = lax.rsqrt(jnp.mean(values * values, axis=-1, keepdims=True) + norm_eps)
    return (values * factor * gain, factor)


def norm_rows_back(values, factor, gain, incoming):
    scaled = incoming * gain
    inward = factor * scaled - values * factor * factor * factor * jnp.mean(
        scaled * values, axis=-1, keepdims=True
    )
    gain_grad = jnp.sum(incoming * values * factor, axis=0)
    return (inward, gain_grad)


def other_core(values):
    return lax.ppermute(values, "mp", [(0, 1), (1, 0)])


def core_total(partial_sum):
    return partial_sum + other_core(partial_sum)


def scatter_sum(values, order, chip_index, keep_type):
    chips = values.shape[0]
    bits = len(order)
    current = values.reshape((2,) * bits + values.shape[1:])
    left = list(range(bits - 1, -1, -1))
    for bit in order:
        axis = left.index(bit)
        mine = (chip_index >> bit) & 1
        sent = lax.dynamic_index_in_dim(current, 1 - mine, axis, False)
        kept = lax.dynamic_index_in_dim(current, mine, axis, False)
        came = lax.ppermute(sent, "dp", [(chip, chip ^ (1 << bit)) for chip in range(chips)])
        current = kept.astype(wide_type) + came.astype(wide_type)
        left.pop(axis)
        if left:
            current = current.astype(keep_type)
    return current


def gather_kernel(owner, lengths, place, rows, out, sums, *, chips, sub):
    slot = pl.program_id(0)
    block = rows[0]
    out[0] = block
    wide = block.astype(wide_type)
    position = (lax.broadcasted_iota(jnp.int32, wide.shape, 0) * 2 + place[1]) * chips + place[0]
    live = jnp.where(position < lengths[owner[slot]], wide, 0.0)
    sums[0] = jnp.concatenate(
        (
            jnp.sum(live, axis=0, keepdims=True),
            jnp.sum(live * wide, axis=0, keepdims=True),
            jnp.zeros((6, wide.shape[1]), wide_type),
        )
    )


def gather_docs(memory_in, doc_owner, mem_lengths, place, chips):
    docs, sub, width = memory_in.shape
    return pl.pallas_call(
        partial(gather_kernel, chips=chips, sub=sub),
        grid_spec=pltpu.PrefetchScalarGridSpec(
            num_scalar_prefetch=3,
            grid=(docs,),
            in_specs=[pl.BlockSpec((1, sub, width), lambda j, owner, lens, place: (owner[j], 0, 0))],
            out_specs=[
                pl.BlockSpec((1, sub, width), lambda j, owner, lens, place: (j, 0, 0)),
                pl.BlockSpec((1, 8, width), lambda j, owner, lens, place: (j, 0, 0)),
            ],
        ),
        out_shape=[
            jax.ShapeDtypeStruct((docs, sub, width), low_type),
            jax.ShapeDtypeStruct((docs, 8, width), wide_type),
        ],
        compiler_params=pltpu.CompilerParams(vmem_limit_bytes=vmem_budget),
        name="gather_docs",
    )(doc_owner, mem_lengths, place, memory_in)


def spread_kernel(owner, rows, out):
    out[0] = rows[0].astype(wide_type)


def spread_docs(rows, doc_owner):
    docs, sub, width = rows.shape
    return pl.pallas_call(
        spread_kernel,
        grid_spec=pltpu.PrefetchScalarGridSpec(
            num_scalar_prefetch=1,
            grid=(docs,),
            in_specs=[pl.BlockSpec((1, sub, width), lambda j, owner: (j, 0, 0))],
            out_specs=pl.BlockSpec((1, sub, width), lambda j, owner: (owner[j], 0, 0)),
        ),
        out_shape=jax.ShapeDtypeStruct((docs, sub, width), wide_type),
        compiler_params=pltpu.CompilerParams(vmem_limit_bytes=vmem_budget),
        name="spread_docs",
    )(doc_owner, rows)


def chunk_of(chips, sub):
    return min(sub, max(16, 512 // chips))


def live_rows(facts, start, chips, span):
    row = lax.broadcasted_iota(jnp.int32, (chips * span, 1), 0)
    chip, step = row // span, row % span
    return ((start + step) * 2 + facts[1]) * chips + chip < facts[0]


def in_branches(facts, start, chips, span, work, dead=None):
    first = (start * 2 + facts[1]) * chips
    last = ((start + span - 1) * 2 + facts[1]) * chips + chips - 1
    full = last < facts[0]
    none = first >= facts[0]

    @pl.when(full)
    def _():
        work(None)

    @pl.when(jnp.logical_not(full) & jnp.logical_not(none))
    def _():
        work(live_rows(facts, start, chips, span))

    if dead is not None:
        pl.when(none)(dead)


def cross_forward_kernel(
    facts, query_t, rows, weight, top_in, total_in, sum_in, pairs, top, total, gathered, *, chips, span
):
    step = pl.program_id(0)
    half = weight.shape[1] // 2
    width = rows.shape[-1]

    @pl.when(step == 0)
    def _():
        top[...] = top_in[...]
        total[...] = total_in[...]
        gathered[...] = sum_in[...]

    def work(live):
        block = rows[...].reshape(chips * span, width)
        made = dot_wide(block, weight[...]).astype(low_type)
        pairs[...] = made.reshape(chips, span, 2 * half)
        for pair in range(half // 128):
            key_pair = made[:, pair * 128 : pair * 128 + 128]
            value_pair = made[:, half + pair * 128 : half + pair * 128 + 128]
            for side in range(2):
                head = pair * 2 + side
                scores = dot_wide(key_pair, query_t[head])
                if live is not None:
                    scores = jnp.where(live, scores, masked_fill)
                old_top = top[head : head + 1, :]
                new_top = jnp.maximum(old_top, jnp.max(scores, axis=0, keepdims=True))
                weights = jnp.exp(scores - new_top)
                shrink = jnp.exp(old_top - new_top)
                total[head : head + 1, :] = total[head : head + 1, :] * shrink + jnp.sum(
                    weights, axis=0, keepdims=True
                )
                part = dot_rows(value_pair, weights.astype(low_type))
                gathered[head * HD : head * HD + HD, :] = (
                    gathered[head * HD : head * HD + HD, :] * shrink + part[side * HD : side * HD + HD, :]
                )
                top[head : head + 1, :] = new_top

    def dead():
        pairs[...] = jnp.zeros_like(pairs)

    in_branches(facts, step * span, chips, span, work, dead)


def whole(shape):
    return pl.BlockSpec(shape, lambda j, facts: (0,) * len(shape))


def cross_forward(facts, query_t, rows, weight, carry):
    chips, sub, width = rows.shape
    heads, _, queries = query_t.shape
    span = chunk_of(chips, sub)
    stat = (8, queries)
    summed = (heads * HD, queries)
    block = pl.BlockSpec((chips, span, width), lambda j, facts: (0, j, 0))
    pair_block = pl.BlockSpec((chips, span, weight.shape[1]), lambda j, facts: (0, j, 0))
    return pl.pallas_call(
        partial(cross_forward_kernel, chips=chips, span=span),
        grid_spec=pltpu.PrefetchScalarGridSpec(
            num_scalar_prefetch=1,
            grid=(sub // span,),
            in_specs=[
                whole(query_t.shape),
                block,
                whole(weight.shape),
                whole(stat),
                whole(stat),
                whole(summed),
            ],
            out_specs=[pair_block, whole(stat), whole(stat), whole(summed)],
        ),
        out_shape=[
            jax.ShapeDtypeStruct((chips, sub, weight.shape[1]), low_type),
            jax.ShapeDtypeStruct(stat, wide_type),
            jax.ShapeDtypeStruct(stat, wide_type),
            jax.ShapeDtypeStruct(summed, wide_type),
        ],
        compiler_params=pltpu.CompilerParams(vmem_limit_bytes=vmem_budget),
        name="cross_forward",
    )(facts, query_t, rows, weight, *carry)


def cross_backward_kernel(
    facts, query, query_t, grad, grad_t, log_total, inner, pairs, weight_t, pair_grads, row_grads, query_grad,
    held, *, chips, span
):
    step = pl.program_id(0)
    half = weight_t.shape[0] // 2
    width = weight_t.shape[1]

    @pl.when(step == 0)
    def _():
        query_grad[...] = jnp.zeros_like(query_grad)

    def work(live):
        block = pairs[...].reshape(chips * span, 2 * half)
        for pair in range(half // 128):
            key_pair = block[:, pair * 128 : pair * 128 + 128]
            value_pair = block[:, half + pair * 128 : half + pair * 128 + 128]
            key_sum, value_sum = 0.0, 0.0
            for side in range(2):
                head = pair * 2 + side
                scores = dot_wide(key_pair, query_t[head])
                if live is not None:
                    scores = jnp.where(live, scores, masked_fill)
                probs = jnp.exp(scores - log_total[head : head + 1, :])
                grad_probs = dot_wide(value_pair, grad_t[head])
                grad_scores = (probs * (grad_probs - inner[head : head + 1, :])).astype(low_type)
                value_sum = value_sum + dot_wide(probs.astype(low_type), grad[head])
                key_sum = key_sum + dot_wide(grad_scores, query[head])
                part = dot_rows(key_pair, grad_scores)
                query_grad[head * HD : head * HD + HD, :] += part[side * HD : side * HD + HD, :]
            held[:, pair * 128 : pair * 128 + 128] = key_sum.astype(low_type)
            held[:, half + pair * 128 : half + pair * 128 + 128] = value_sum.astype(low_type)
        made = held[...]
        pair_grads[...] = made.reshape(chips, span, 2 * half)
        row_grads[...] = dot_wide(made, weight_t[...]).astype(row_grads.dtype).reshape(chips, span, width)

    def dead():
        pair_grads[...] = jnp.zeros_like(pair_grads)
        row_grads[...] = jnp.zeros_like(row_grads)

    in_branches(facts, step * span, chips, span, work, dead)


def cross_backward(facts, query, query_t, grad, grad_t, log_total, inner, pairs, weight_t, grad_type):
    chips, sub, both = pairs.shape
    width = weight_t.shape[1]
    heads, _, queries = query_t.shape
    span = chunk_of(chips, sub)
    pair_block = pl.BlockSpec((chips, span, both), lambda j, facts: (0, j, 0))
    row_block = pl.BlockSpec((chips, span, width), lambda j, facts: (0, j, 0))
    return pl.pallas_call(
        partial(cross_backward_kernel, chips=chips, span=span),
        grid_spec=pltpu.PrefetchScalarGridSpec(
            num_scalar_prefetch=1,
            grid=(sub // span,),
            in_specs=[
                whole(query.shape),
                whole(query_t.shape),
                whole(grad.shape),
                whole(grad_t.shape),
                whole(log_total.shape),
                whole(inner.shape),
                pair_block,
                whole(weight_t.shape),
            ],
            out_specs=[pair_block, row_block, whole((heads * HD, queries))],
            scratch_shapes=[pltpu.VMEM((chips * span, both), low_type)],
        ),
        out_shape=[
            jax.ShapeDtypeStruct((chips, sub, both), low_type),
            jax.ShapeDtypeStruct((chips, sub, width), grad_type),
            jax.ShapeDtypeStruct((heads * HD, queries), wide_type),
        ],
        compiler_params=pltpu.CompilerParams(vmem_limit_bytes=vmem_budget),
        name="cross_backward",
    )(facts, query, query_t, grad, grad_t, log_total, inner, pairs, weight_t)


def padded_heads(values):
    rows, width = values.shape
    pairs = values.reshape(rows, width // 128, 128).transpose(1, 0, 2)
    left = lax.broadcasted_iota(jnp.int32, (1, 1, 128), 2) < HD
    none = jnp.zeros_like(pairs)
    both = jnp.stack((jnp.where(left, pairs, none), jnp.where(left, none, pairs)), axis=1)
    return both.reshape(width // HD, rows, 128)


def padded_heads_t(values_t):
    width, rows = values_t.shape
    pairs = values_t.reshape(width // 128, 2, HD, rows)
    none = jnp.zeros_like(pairs[:, 0])
    even = jnp.concatenate((pairs[:, 0], none), axis=1)
    odd = jnp.concatenate((none, pairs[:, 1]), axis=1)
    return jnp.stack((even, odd), axis=1).reshape(width // HD, 128, rows)


def attend(queries, key_rows, values, allowed):
    scores = (
        jnp.einsum("hne,hme->hnm", queries, key_rows, preferred_element_type=jnp.float32) * 0.125
    )
    scores = jnp.where(allowed, scores, masked_fill)
    row_max = jnp.max(scores, axis=-1, keepdims=True)
    shifted = jnp.exp(scores - row_max)
    row_total = jnp.sum(shifted, axis=-1, keepdims=True)
    weights = (shifted / row_total).astype(jnp.bfloat16)
    output = jnp.einsum("hnm,hme->hne", weights, values, preferred_element_type=jnp.float32)
    return (output.astype(jnp.bfloat16), (row_max + jnp.log(row_total))[..., 0])


def attend_back(queries, key_rows, values, allowed, log_total, grad_output):
    scores = (
        jnp.einsum("hne,hme->hnm", queries, key_rows, preferred_element_type=jnp.float32) * 0.125
    )
    scores = jnp.where(allowed, scores, masked_fill)
    probs = jnp.exp(scores - log_total[..., None])
    grad_probs = jnp.einsum("hne,hme->hnm", grad_output, values, preferred_element_type=jnp.float32)
    grad_scores = probs * (grad_probs - jnp.sum(probs * grad_probs, axis=-1, keepdims=True))
    grad_low = grad_scores.astype(jnp.bfloat16)
    query_grad = (
        jnp.einsum("hnm,hme->hne", grad_low, key_rows, preferred_element_type=jnp.float32) * 0.125
    )
    key_grad = (
        jnp.einsum("hnm,hne->hme", grad_low, queries, preferred_element_type=jnp.float32) * 0.125
    )
    value_grad = jnp.einsum(
        "hnm,hne->hme", probs.astype(jnp.bfloat16), grad_output, preferred_element_type=jnp.float32
    )
    return (query_grad, key_grad, value_grad)


def shards(
    dec_input,
    out_grad,
    enc_feats,
    mem_lengths,
    dec_lengths,
    doc_owner,
    group_gain,
    group_bias,
    conv_weight,
    cross_kv,
    self_gain,
    self_qkv,
    self_out,
    cross_gain,
    cross_query,
    cross_out,
    ffn_gain,
    ffn_in,
    ffn_out,
):
    chips = lax.axis_size("dp")
    chip_index = lax.axis_index("dp")
    core_index = lax.axis_index("mp")
    memory_in = enc_feats[0, 0]
    docs, sub, width = memory_in.shape
    per_group = width // GROUPS
    half = width // 2
    heads = half // HD
    rows_here = docs * sub
    share = width // chips
    bits = chips.bit_length() - 1
    orders = [
        tuple((bit + turn) % 3 if bit < 3 else bit for bit in range(bits)) if bits >= 3 else tuple(range(bits))
        for turn in range(3)
    ]

    place = jnp.stack((chip_index, core_index)).astype(jnp.int32)
    outgoing, channel_sums = gather_docs(memory_in, doc_owner, mem_lengths, place, chips)
    features = lax.all_to_all(outgoing, "dp", split_axis=0, concat_axis=0, tiled=True)
    group_of = (
        lax.broadcasted_iota(jnp.int32, (width, GROUPS), 0) // per_group
        == lax.broadcasted_iota(jnp.int32, (width, GROUPS), 1)
    ).astype(wide_type)

    def group_sums(channels):
        return jnp.dot(channels, group_of, precision=lax.Precision.HIGHEST)

    def to_channels(groups):
        return jnp.dot(groups, group_of.T, precision=lax.Precision.HIGHEST)

    sums_here = group_sums(channel_sums[:, :2].reshape(docs * 2, width)).reshape(docs, 2 * GROUPS)
    sums_all = core_total(scatter_sum(sums_here, orders[0], chip_index, wide_type))
    document = doc_owner[chip_index]
    length = mem_lengths[document]
    entries = (length * per_group).astype(wide_type)
    center = sums_all[:GROUPS] / entries
    spread = lax.rsqrt(sums_all[GROUPS:] / entries - center * center + group_eps)
    channel_stats = to_channels(jnp.stack((center, spread)))
    center_row, spread_row = channel_stats[0:1], channel_stats[1:2]

    dec_rows = DEC
    input_flat = dec_input.astype(wide_type).reshape(dec_rows, width)
    normed_one, factor_one = norm_rows(input_flat, self_gain)
    normed_one = normed_one.astype(low_type)
    self_weight = self_qkv.reshape(width, 3 * half)
    qkv_self = dot_wide(normed_one, self_weight).astype(low_type)
    qkv_heads = qkv_self.reshape(DEC, 3, heads, HD).transpose(1, 2, 0, 3)
    row_pos = lax.broadcasted_iota(jnp.int32, (DEC, DEC), 0)
    col_pos = lax.broadcasted_iota(jnp.int32, (DEC, DEC), 1)
    allowed = ((col_pos <= row_pos) & (col_pos < dec_lengths[chip_index]))[None]
    output, self_total = attend(qkv_heads[0], qkv_heads[1], qkv_heads[2], allowed)
    attended = output.transpose(1, 0, 2).reshape(dec_rows, half)
    first_out = input_flat + core_total(dot_wide(attended, self_out))
    normed_two, factor_two = norm_rows(first_out, cross_gain)
    normed_two = normed_two.astype(low_type)
    cross_q = dot_wide(normed_two, cross_query).astype(low_type) * jnp.asarray(0.125, low_type)
    query_heads = padded_heads(cross_q)
    query_heads_t = padded_heads_t(cross_q.T)

    features_wide = features.reshape(rows_here, width).astype(wide_type)
    normed = (features_wide - center_row) * spread_row
    activation_in = normed * group_gain + group_bias
    hidden = jax.nn.silu(activation_in).astype(low_type)
    memory_own = (features_wide + dot_wide(hidden, conv_weight)).astype(low_type)
    memory_other = other_core(memory_own)
    pair_weight = lax.dynamic_slice_in_dim(cross_kv, core_index * half, half, axis=2).reshape(width, 2 * half)

    facts_own = jnp.stack((length, core_index)).astype(jnp.int32)
    facts_other = jnp.stack((length, 1 - core_index)).astype(jnp.int32)
    carry = (
        jnp.full((8, dec_rows), -1e30, wide_type),
        jnp.zeros((8, dec_rows), wide_type),
        jnp.zeros((half, dec_rows), wide_type),
    )
    pairs_own, *carry = cross_forward(
        facts_own, query_heads_t, memory_own.reshape(chips, sub, width), pair_weight, carry
    )
    pairs_other, top, total, gathered = cross_forward(
        facts_other, query_heads_t, memory_other.reshape(chips, sub, width), pair_weight, carry
    )
    crossed_t = (gathered.reshape(heads, HD, dec_rows) / total[:heads, None, :]).reshape(half, dec_rows)
    log_total = top + jnp.log(jnp.maximum(total, 1e-30))
    crossed = crossed_t.T.astype(low_type)
    second_out = first_out + core_total(dot_wide(crossed, cross_out))

    normed_three, factor_three = norm_rows(second_out, ffn_gain)
    normed_three = normed_three.astype(low_type)
    lifted = dot_wide(normed_three, ffn_in)
    gelu_value, gelu_back = jax.vjp(partial(jax.nn.gelu, approximate=True), lifted)
    active = gelu_value.astype(low_type)
    grad_low = out_grad.reshape(dec_rows, width)
    grad_result = grad_low.astype(wide_type)
    grad_active = dot_columns(grad_low, ffn_out).astype(low_type)
    grad_lifted = gelu_back(grad_active.astype(wide_type))[0].astype(low_type)
    grad_normed_three = core_total(dot_columns(grad_lifted, ffn_in))
    grad_second, ffn_gain_grad = norm_rows_back(second_out, factor_three, ffn_gain, grad_normed_three)
    grad_second = grad_second + grad_result
    grad_cross = grad_second.astype(low_type)
    grad_crossed = dot_columns(grad_cross, cross_out).astype(low_type)
    grad_crossed_t = grad_crossed.T
    inner = jnp.sum(
        (grad_crossed_t.astype(wide_type) * crossed_t).reshape(heads, HD, dec_rows), axis=1
    )
    inner = jnp.concatenate((inner, jnp.zeros((8 - heads, dec_rows), wide_type)))
    grad_heads = padded_heads(grad_crossed)
    grad_heads_t = padded_heads_t(grad_crossed_t)

    result = second_out + core_total(dot_wide(active, ffn_out))
    layer_out = result.astype(low_type).reshape(1, DEC, width)

    def by_row(grad):
        return grad.astype(low_type).reshape(chips, share, grad.shape[1])

    third = 2 * active.shape[1] // 3
    ffn_parts = (
        scatter_sum(by_row(dot_rows(normed_three, grad_lifted[:, :third])), orders[0], chip_index, low_type),
        scatter_sum(by_row(dot_rows(normed_three, grad_lifted[:, third:])), orders[1], chip_index, low_type),
        scatter_sum(by_row(dot_rows(grad_low, active[:, : third // 2])), orders[1], chip_index, low_type),
        scatter_sum(by_row(dot_rows(grad_low, active[:, third // 2 :])), orders[2], chip_index, low_type),
    )
    ffn_in_grad = jnp.concatenate(ffn_parts[:2], axis=1)
    ffn_out_grad = jnp.concatenate(ffn_parts[2:], axis=1).T

    weight_t = pair_weight.T
    pair_grads_other, row_grads_other, query_grad_other = cross_backward(
        facts_other, query_heads, query_heads_t, grad_heads, grad_heads_t, log_total, inner, pairs_other, weight_t,
        low_type,
    )
    row_grads_came = other_core(row_grads_other)
    pair_grads_own, row_grads_own, query_grad_own = cross_backward(
        facts_own, query_heads, query_heads_t, grad_heads, grad_heads_t, log_total, inner, pairs_own, weight_t,
        wide_type,
    )
    grad_memory = (row_grads_own + row_grads_came.astype(wide_type)).astype(low_type).reshape(rows_here, width)

    grad_hidden = dot_columns(grad_memory, conv_weight)
    gate = jax.nn.sigmoid(activation_in)
    grad_act = grad_hidden * gate * (1.0 + activation_in * (1.0 - gate))
    gain_part = jnp.sum(grad_act * normed, axis=0)
    bias_part = jnp.sum(grad_act, axis=0)
    backs = to_channels(group_sums(core_total(jnp.stack((bias_part, gain_part))) * group_gain)) / entries
    position = (
        (lax.broadcasted_iota(jnp.int32, (chips, sub, 1), 1) * 2 + core_index) * chips
        + lax.broadcasted_iota(jnp.int32, (chips, sub, 1), 0)
    ).reshape(rows_here, 1)
    live = (position < length).astype(wide_type)
    grad_features = grad_memory.astype(wide_type) + spread_row * (
        grad_act * group_gain - live * (backs[0:1] + normed * backs[1:2])
    )
    returned = lax.all_to_all(
        grad_features.astype(low_type).reshape(docs, sub, width), "dp", split_axis=0, concat_axis=0, tiled=True
    )
    memory_grad = spread_docs(returned, doc_owner).reshape(1, 1, docs, sub, width)

    grad_cq = ((query_grad_own + query_grad_other) * 0.125).T.astype(low_type)
    grad_normed_two = core_total(dot_columns(grad_cq, cross_query))
    grad_first, cross_gain_grad = norm_rows_back(first_out, factor_two, cross_gain, grad_normed_two)
    grad_first = grad_first + grad_second
    grad_self = grad_first.astype(low_type)
    grad_attended = dot_columns(grad_self, self_out).astype(low_type)
    grad_attended = grad_attended.reshape(DEC, heads, HD).transpose(1, 0, 2)
    query_grad, key_grad, value_grad = attend_back(
        qkv_heads[0], qkv_heads[1], qkv_heads[2], allowed, self_total, grad_attended
    )
    grad_qkv = (
        jnp.stack((query_grad, key_grad, value_grad))
        .astype(low_type)
        .transpose(2, 0, 1, 3)
        .reshape(dec_rows, 3 * half)
    )
    grad_normed_one = core_total(dot_columns(grad_qkv, self_weight))
    grad_input, self_gain_grad = norm_rows_back(input_flat, factor_one, self_gain, grad_normed_one)
    input_grad = (grad_input + grad_first).reshape(1, DEC, width)

    pair_weight_grad = dot_rows(memory_own, pair_grads_own.reshape(rows_here, 2 * half)) + dot_rows(
        memory_other, pair_grads_other.reshape(rows_here, 2 * half)
    )
    conv_part = dot_rows(hidden, grad_memory)
    conv_keep = lax.dynamic_slice_in_dim(conv_part, core_index * half, half, axis=1)
    conv_send = lax.dynamic_slice_in_dim(conv_part, (1 - core_index) * half, half, axis=1).astype(low_type)
    conv_half = conv_keep + other_core(conv_send).astype(wide_type)
    pair_sum = scatter_sum(by_row(pair_weight_grad), orders[0], chip_index, low_type)
    conv_sum = scatter_sum(by_row(conv_half), orders[1], chip_index, low_type)
    cross_out_sum = scatter_sum(by_row(dot_rows(grad_cross, crossed)), orders[2], chip_index, low_type)
    cross_query_sum = scatter_sum(by_row(dot_rows(normed_two, grad_cq)), orders[2], chip_index, low_type)
    self_out_sum = scatter_sum(by_row(dot_rows(grad_self, attended)), orders[2], chip_index, low_type)
    self_qkv_sum = scatter_sum(by_row(dot_rows(normed_one, grad_qkv)), orders[1], chip_index, low_type)
    gains = jnp.stack((gain_part, bias_part, self_gain_grad, cross_gain_grad, ffn_gain_grad))
    gains = jnp.concatenate((gains, jnp.zeros((3, width), wide_type)))
    gain_sums = scatter_sum(
        gains.reshape(8, chips, share).transpose(1, 0, 2), orders[0], chip_index, wide_type
    )
    group_sums_both = core_total(gain_sums[:2])

    def both_cores(mine):
        theirs = other_core(mine.astype(low_type)).astype(wide_type)
        return jnp.where(core_index == 0, mine, theirs), jnp.where(core_index == 0, theirs, mine)

    conv_grad = jnp.concatenate(both_cores(conv_sum), axis=1)
    pair_left, pair_right = both_cores(pair_sum)
    cross_kv_grad = jnp.concatenate(
        (pair_left.reshape(share, 2, half), pair_right.reshape(share, 2, half)), axis=2
    )
    return (
        layer_out,
        input_grad,
        memory_grad,
        group_sums_both[0],
        group_sums_both[1],
        conv_grad,
        cross_kv_grad,
        gain_sums[2],
        self_qkv_sum.reshape(share, 3, half),
        self_out_sum.T,
        gain_sums[3],
        cross_query_sum,
        cross_out_sum.T,
        gain_sums[4],
        ffn_in_grad,
        ffn_out_grad,
    )


def solution(mesh):
    placed = (
        P("dp", None, None),
        P("dp", None, None),
        P("dp", "mp", None, None, None),
        P(),
        P(),
        P(),
        P(),
        P(),
        P(),
        P(),
        P(),
        P(None, None, "mp"),
        P("mp", None),
        P(),
        P(None, "mp"),
        P("mp", None),
        P(),
        P(None, "mp"),
        P("mp", None),
    )
    return jax.shard_map(
        shards,
        mesh=mesh,
        in_specs=placed,
        out_specs=(
            P("dp", None, None),
            P("dp", None, None),
            P("dp", "mp", None, None, None),
            P("dp"),
            P("dp"),
            P("dp", None),
            P("dp", None, None),
            P("dp"),
            P("dp", None, "mp"),
            P("mp", "dp"),
            P("dp"),
            P("dp", "mp"),
            P("mp", "dp"),
            P("dp"),
            P("dp", "mp"),
            P("mp", "dp"),
        ),
        check_vma=False,
    )
```

time: 2090 us -> 592 us (0.28)
  waiting for transfers between devices: 1140 us -> 201 us
  local copies, waits for them, and re-layouts: 268 us -> 54.9 us
  blocking collectives: 210 us -> 0 us
  matrix products: 265 us -> 78.5 us
  starting transfers between devices: 14.1 us -> 116 us
  other arithmetic: 156 us -> 66.8 us
  Pallas kernels: 0 us -> 57.2 us
    reduce_scatter x7 -> x0, waiting for transfers between devices: 827 us -> none  [the longest x1 143 us: shards(): lax.psum_scatter(ffn_in_grad, 'dp', scatter_dimension=0, tiled=True)]
    ppermute x0 -> x62, waiting for transfers between devices: none -> 201 us  [the longest x48 201 us: scatter_sum(): lax.ppermute(sent, 'dp', [(chip, chip ^ 1 << bit) for chip in range(chips)])]
    psum x4 -> x0, waiting for transfers between devices: 121 us -> none  [the longest x3 73.6 us: head_total(): return lax.psum(partial_sum, 'mp')]
    all_to_all x1, waiting for transfers between devices: 119 us -> 0.01 us  [shards(): lax.all_to_all(grad_features.astype(low_type).reshape(docs, sub, width),...]
    psum x6 -> x0, blocking collectives: 113 us -> none  [the longest x1 42.6 us: shards(): first_sum, second_sum = lax.psum((first_sum, second_sum), ('dp', 'mp'))]
    ppermute x0 -> x62, starting transfers between devices: none -> 104 us  [the longest x48 103 us: scatter_sum(): lax.ppermute(sent, 'dp', [(chip, chip ^ 1 << bit) for chip in range(chips)])]
    all_to_all x1, waiting for transfers between devices: 76.5 us -> 0.01 us  [shards(): lax.all_to_all(outgoing, 'dp', split_axis=0, concat_axis=0, tiled=True)]
    unnamed x1 -> x0, blocking collectives: 75.7 us -> none
  transfers between devices with their start and end apart: 14 -> 64, of which waited for: 13 -> 31; matrix products, arithmetic and copies ran while one was open for 8% -> 24% of each run, Pallas kernels for 0% -> 2%
where the time goes in v1:
time: 592 us; the launch traced here: 581 us
  waiting for transfers between devices  201 us (34%)
  starting transfers between devices  116 us (20%)
  matrix products  78.5 us (13%)
  other arithmetic  66.8 us (11%)
  Pallas kernels  57.2 us (10%)
  local copies, waits for them, and re-layouts  54.9 us (9%)
    ppermute x48, waiting for transfers between devices, scatter_sum(): lax.ppermute(sent, 'dp', [(chip, chip ^ 1 << bit) for chip in range(chips)])  201 us
    ppermute x48, starting transfers between devices, scatter_sum(): lax.ppermute(sent, 'dp', [(chip, chip ^ 1 << bit) for chip in range(chips)])  103 us
    dot_general x11, matrix products, dot_rows(): lax.dot_general(left, right, (((0,), (0,)), ((), ())), preferred_element_...  26.4 us
    pallas_call x2, Pallas kernels, cross_backward(): pl.pallas_call(partial(cross_backward_kernel, chips=chips, span=span), gr...  23 us
    unnamed x215, local copies, waits for them, and re-layouts  22.7 us
    dot_general x7, matrix products, dot_columns(): lax.dot_general(left, right, (((1,), (1,)), ((), ())), preferred_element_...  19 us
    pallas_call x2, Pallas kernels, cross_forward(): pl.pallas_call(partial(cross_forward_kernel, chips=chips, span=span), gri...  18.1 us
    dot_general x7, matrix products, dot_wide(): return jnp.dot(left, right, preferred_element_type=wide_type)  17.7 us
  transfers between devices with their start and end apart: 64, of which 31 were waited for; matrix products, arithmetic and copies ran while one was open for 24% of the time, Pallas kernels for 2%

profile of v1, /device:TPU:0, one launch (start us, length us, event | category | flops | bytes accessed | tf_op | source)
XLA Modules:
  0.0 580.7 jit_solution(7624051991029786318)
XLA Ops:
  2.2 9.1 %gather_docs.1 = (bf16[16,128,768]{2,1,0:T(8,128)(2,1)S(1)}, f32[16,8,768]{2,1,0:T(8,128)S(1)}) custom-call(s32[16]{0:T(128)S(1)} %copy-done.10, s32[16]{0:T(128)S(1)} %copy-done.12, s32[2]{0:T(128)S(1)} %pad_add_fusion.1.place, bf16[16,128,768]{2,1,0:T(8,128)(2,1)} %bitcast.610), custom_call_target="tpu_custom_call" | custom-call | tf_op jit(solution)/shard_map/gather_docs/pallas_call | solution.py:93
  13.1 8.4 %all-to-all-start = ((bf16[16,128,768]{2,1,0:T(8,128)(2,1)}), bf16[16,128,768]{2,1,0:T(8,128)(2,1)}, u32[]{:S(2)}, u32[]{:S(2)}) async-start(bf16[16,128,768]{2,1,0:T(8,128)(2,1)} %copy-done.7), calls=%async_computation | async-start | bytes 6291456 | tf_op jit(solution)/shard_map/all_to_all | solution.py:412
  25.3 3.9 copy.150
  30.1 3.7 convolution_convert_fusion.1
  36.9 3.9 fusion.176
  43.0 3.6 fusion.31
  48.4 4.0 fusion.78
  53.0 20.4 %collective-permute-done.3 = f32[2,64]{1,0:T(2,128)S(1)} collective-permute-done((f32[2,64]{1,0:T(2,128)S(1)}, f32[2,64]{1,0:T(2,128)S(1)}, u32[]{:S(2)}, u32[]{:S(2)}) %collective-permute-start.3) | collective-permute-done | bytes 544 | tf_op jit(solution)/shard_map/ppermute | solution.py:67
  73.5 3.3 collective-permute-start.4
  78.8 13.3 %collective-permute-done.4 = f32[64]{0:T(128)S(1)} collective-permute-done((f32[64]{0:T(128)S(1)}, f32[64]{0:T(128)S(1)}, u32[]{:S(2)}, u32[]{:S(2)}) %collective-permute-start.4) | collective-permute-done | bytes 288 | tf_op jit(solution)/shard_map/ppermute | solution.py:67
  94.5 3.8 fusion.20
  98.3 5.4 fusion.30
  106.0 3.1 constant_dynamic-slice_fusion.22
  109.1 3.6 copy.157
  120.6 8.9 %cross_forward.2 = (bf16[16,128,768]{2,1,0:T(8,128)(2,1)}, f32[8,512]{1,0:T(8,128)S(1)}, f32[8,512]{1,0:T(8,128)S(1)}, f32[384,512]{1,0:T(8,128)S(1)}) custom-call(s32[2]{0:T(128)S(1)} %pad_add_fusion.2.facts, bf16[6,128,512]{2,1,0:T(8,128)(2,1)S(1)} %bitcast.573, bf16[16,128,768]{2,1,0:T(8,128)(2,1)} %bitcast.39.rows, bf16[768,768]{1,0:T(8,128)(2,1)S(1)} %copy-done.6, ...), custom_call_target="tpu_custom_call" | custom-call | tf_op jit(solution)/shard_map/cross_forward/pallas_call | solution.py:217
  129.5 9.2 %cross_forward.3 = (bf16[16,128,768]{2,1,0:T(8,128)(2,1)}, f32[8,512]{1,0:T(8,128)S(1)}, f32[8,512]{1,0:T(8,128)S(1)}, f32[384,512]{1,0:T(8,128)S(1)}) custom-call(s32[2]{0:T(128)S(1)} %pad_add_fusion.facts, bf16[6,128,512]{2,1,0:T(8,128)(2,1)S(1)} %bitcast.574, bf16[16,128,768]{2,1,0:T(8,128)(2,1)} %bitcast.37.rows, bf16[768,768]{1,0:T(8,128)(2,1)S(1)} %copy-done.6, ...), custom_call_target="tpu_custom_call" | custom-call | tf_op jit(solution)/shard_map/cross_forward/pallas_call | solution.py:217
  146.3 2.6 multiply_reduce_fusion.5
  154.9 3.2 fusion.35
  159.6 2.7 fusion.180
  165.1 21.9 %collective-permute-start.54 = (bf16[2,2,2,48,512]{4,3,2,1,0:T(8,128)(2,1)S(1)}, bf16[2,2,2,48,512]{4,3,2,1,0:T(8,128)(2,1)S(1)}, u32[]{:S(2)}, u32[]{:S(2)}) collective-permute-start(bf16[2,2,2,48,512]{4,3,2,1,0:T(8,128)(2,1)S(1)} %dynamic-slice_bitcast_fusion.3), channel_id=1, source_target_pairs={{0,4},{2,6},{4,0},{6,2},{8,12},{10,14},{12,8},{14,10},{16,20},{18,... | collective-permute-start | bytes 1179656 | tf_op jit(solution)/shard_map/ppermute | solution.py:67
  192.7 4.2 collective-permute-done.54
  197.1 7.6 %collective-permute-done.50 = bf16[2,2,2,48,512]{4,3,0,2,1:T(8,128)(2,1)S(1)} collective-permute-done((bf16[2,2,2,48,512]{4,3,0,2,1:T(8,128)(2,1)S(1)}, bf16[2,2,2,48,512]{4,3,0,2,1:T(8,128)(2,1)S(1)}, u32[]{:S(2)}, u32[]{:S(2)}) %collective-permute-start.50) | collective-permute-done | bytes 393248 | tf_op jit(solution)/shard_map/ppermute | solution.py:67
  204.9 7.3 %collective-permute-done.55 = bf16[2,2,48,512]{3,2,1,0:T(8,128)(2,1)S(1)} collective-permute-done((bf16[2,2,48,512]{3,2,1,0:T(8,128)(2,1)S(1)}, bf16[2,2,48,512]{3,2,1,0:T(8,128)(2,1)S(1)}, u32[]{:S(2)}, u32[]{:S(2)}) %collective-permute-start.55) | collective-permute-done | bytes 196640 | tf_op jit(solution)/shard_map/ppermute | solution.py:67
  212.6 5.4 collective-permute-done.51
  218.1 5.0 collective-permute-done.56
  223.2 4.6 collective-permute-done.52
  227.8 5.2 collective-permute-done.57
  234.6 3.3 collective-permute-done.53
  238.0 3.2 collective-permute-done.59
  244.5 2.6 collective-permute-done.60
  247.2 3.0 collective-permute-start.61
  252.8 4.6 collective-permute-done.49
  269.1 10.9 %cross_backward.3 = (bf16[16,128,768]{2,1,0:T(8,128)(2,1)}, bf16[16,128,768]{2,1,0:T(8,128)(2,1)}, f32[384,512]{1,0:T(8,128)S(1)}) custom-call(s32[2]{0:T(128)S(1)} %pad_add_fusion.facts, bf16[6,512,128]{2,1,0:T(8,128)(2,1)S(1)} %bitcast.580, bf16[6,128,512]{2,1,0:T(8,128)(2,1)S(1)} %bitcast.575, bf16[6,512,128]{2,1,0:T(8,128)(2,1)S(1)} %bitcast.584, ...), custom_call_target="tpu_custom_call" | custom-call | tf_op jit(solution)/shard_map/cross_backward/pallas_call | solution.py:293
  280.0 12.1 %cross_backward.2 = (bf16[16,128,768]{2,1,0:T(8,128)(2,1)}, f32[16,128,768]{2,1,0:T(8,128)}, f32[384,512]{1,0:T(8,128)S(1)}) custom-call(s32[2]{0:T(128)S(1)} %pad_add_fusion.2.facts, bf16[6,512,128]{2,1,0:T(8,128)(2,1)S(1)} %bitcast.581, bf16[6,128,512]{2,1,0:T(8,128)(2,1)S(1)} %bitcast.576, bf16[6,512,128]{2,1,0:T(8,128)(2,1)S(1)} %bitcast.585, ...), custom_call_target="tpu_custom_call" | custom-call | tf_op jit(solution)/shard_map/cross_backward/pallas_call | solution.py:293
  301.5 4.8 fusion.183
  306.3 4.7 add_convert_fusion.1
  311.9 25.0 %collective-permute-start.25 = (bf16[2,2,2,48,768]{4,3,2,1,0:T(8,128)(2,1)}, bf16[2,2,2,48,768]{4,3,2,1,0:T(8,128)(2,1)}, u32[]{:S(2)}, u32[]{:S(2)}) collective-permute-start(bf16[2,2,2,48,768]{4,3,2,1,0:T(8,128)(2,1)} %dynamic-slice_bitcast_fusion), channel_id=1, source_target_pairs={{0,2},{2,0},{4,6},{6,4},{8,10},{10,8},{12,14},{14,12},{16,18},{18,... | collective-permute-start | bytes 1769480 | tf_op jit(solution)/shard_map/ppermute | solution.py:67
  342.2 12.3 %collective-permute-done.43 = bf16[2,2,48,384]{3,2,0,1:T(8,128)(2,1)S(1)} collective-permute-done((bf16[2,2,48,384]{3,2,0,1:T(8,128)(2,1)S(1)}, bf16[2,2,48,384]{3,2,0,1:T(8,128)(2,1)S(1)}, u32[]{:S(2)}, u32[]{:S(2)}) %collective-permute-start.43) | collective-permute-done | bytes 147488 | tf_op jit(solution)/shard_map/ppermute | solution.py:67
  354.5 2.9 collective-permute-start.44
  357.5 2.7 collective-permute-start.40
  363.3 3.0 collective-permute-start.41
  366.2 3.8 collective-permute-done.26
  371.7 3.6 collective-permute-done.27
  375.4 3.5 collective-permute-start.28
  383.1 3.1 multiply_reduce_fusion.2
  402.2 5.3 collective-permute-done.34
  416.3 8.1 %collective-permute-done.30 = bf16[2,2,2,48,1152]{4,3,0,2,1:T(8,128)(2,1)} collective-permute-done((bf16[2,2,2,48,1152]{4,3,0,2,1:T(8,128)(2,1)}, bf16[2,2,2,48,1152]{4,3,0,2,1:T(8,128)(2,1)}, u32[]{:S(2)}, u32[]{:S(2)}) %collective-permute-start.30) | collective-permute-done | bytes 884768 | tf_op jit(solution)/shard_map/ppermute | solution.py:67
  433.5 5.8 %collective-permute-done.31 = bf16[2,2,48,1152]{3,2,0,1:T(8,128)(2,1)} collective-permute-done((bf16[2,2,48,1152]{3,2,0,1:T(8,128)(2,1)}, bf16[2,2,48,1152]{3,2,0,1:T(8,128)(2,1)}, u32[]{:S(2)}, u32[]{:S(2)}) %collective-permute-start.31) | collective-permute-done | bytes 442400 | tf_op jit(solution)/shard_map/ppermute | solution.py:67
  441.9 4.8 collective-permute-done.32
  449.4 4.6 add_convert_fusion
  454.1 9.2 %fusion.174 = (f32[768]{0:T(1024)S(1)}, f32[768]{0:T(1024)S(1)}, f32[2048,768]{1,0:T(8,128)}) fusion(f32[768]{0:T(1024)S(1)} %copy-done.75, f32[768]{0:T(1024)S(1)} %copy-done.73, bf16[16,128,768]{2,1,0:T(8,128)(2,1)} %all-to-all-done, f32[768]{0:T(1024)S(1)} %copy-done.87, f32[768]{0:T(1024)S(1)} %copy-done.82, bf16[2048,768]{1,0:T(8,128)(2,1)S(1)} %bitcast.591, ...), kind=kOutput, calls=%fused_computation.400 | convolution fusion | flops 2441083392 | bytes 13780992 | tf_op jit(solution)/shard_map/dot_general | solution.py:32
  468.5 7.2 %fusion.29 = bf16[2048,768]{1,0:T(8,128)(2,1)} fusion(bf16[16,128,768]{2,1,0:T(8,128)(2,1)} %all-to-all-done, f32[2048,768]{1,0:T(8,128)} %get-tuple-element.165, f32[768]{0:T(1024)S(1)} %get-tuple-element.105, f32[768]{0:T(1024)S(1)} %get-tuple-element.104, f32[2048]{0:T(1024)S(1)} %copy-done.77, f32[768]{0:T(1024)S(1)} %copy-done.82, ...), kind=kLoop, calls=%fused_computation.32 | loop fusion | flops 18874368 | bytes 15752192 | tf_op jit(solution)/shard_map/convert_element_type | solution.py:544
  475.7 3.7 all-to-all-start.1
  479.4 6.4 %fusion.55 = f32[768,768]{1,0:T(8,128)S(1)} fusion(bf16[16,128,768]{2,1,0:T(8,128)(2,1)} %copy-done.24, bf16[16,128,768]{2,1,0:T(8,128)(2,1)} %all-to-all-done, f32[768]{0:T(1024)S(1)} %copy-done.87, f32[768]{0:T(1024)S(1)} %copy-done.82, f32[768]{0:T(1024)S(1)} %copy-done.75, f32[768]{0:T(1024)S(1)} %copy-done.73), kind=kOutput, calls=%fused_computation.75 | convolution fusion | flops 2431647744 | bytes 8663040 | tf_op jit(solution)/shard_map/dot_general | solution.py:28
  487.9 8.4 %collective-permute-done.15 = f32[2,2,8,48]{3,2,1,0:T(8,128)S(1)} collective-permute-done((f32[2,2,8,48]{3,2,1,0:T(8,128)S(1)}, f32[2,2,8,48]{3,2,1,0:T(8,128)S(1)}, u32[]{:S(2)}, u32[]{:S(2)}) %collective-permute-start.15) | collective-permute-done | bytes 6176 | tf_op jit(solution)/shard_map/ppermute | solution.py:67
  496.7 35.4 %collective-permute-done.16 = f32[2,8,48]{2,1,0:T(8,128)S(1)} collective-permute-done((f32[2,8,48]{2,1,0:T(8,128)S(1)}, f32[2,8,48]{2,1,0:T(8,128)S(1)}, u32[]{:S(2)}, u32[]{:S(2)}) %collective-permute-start.16) | collective-permute-done | bytes 3104 | tf_op jit(solution)/shard_map/ppermute | solution.py:67
  532.2 3.5 collective-permute-start.17
  535.9 3.6 collective-permute-start.20
  539.5 3.2 fusion.64
  542.7 8.2 %collective-permute-done.17 = f32[8,48]{1,0:T(8,128)S(1)} collective-permute-done((f32[8,48]{1,0:T(8,128)S(1)}, f32[8,48]{1,0:T(8,128)S(1)}, u32[]{:S(2)}, u32[]{:S(2)}) %collective-permute-start.17) | collective-permute-done | bytes 1568 | tf_op jit(solution)/shard_map/ppermute | solution.py:67
  551.6 5.7 collective-permute-done.21
  557.4 2.6 collective-permute-start.22
  563.8 3.6 collective-permute-done.23
  573.4 6.9 %spread_docs.1 = f32[16,128,768]{2,1,0:T(8,128)} custom-call(s32[16]{0:T(128)S(1)} %copy-done.11, bf16[16,128,768]{2,1,0:T(8,128)(2,1)S(1)} %copy-done.5), custom_call_target="tpu_custom_call" | custom-call | tf_op jit(solution)/shard_map/spread_docs/pallas_call | solution.py:119
  (520 shorter events, 152.2 us)
Async XLA Ops:
  13.1 81.4 %all-to-all-start = ((bf16[16,128,768]{2,1,0:T(8,128)(2,1)}), bf16[16,128,768]{2,1,0:T(8,128)(2,1)}, u32[]{:S(2)}, u32[]{:S(2)}) async-start(bf16[16,128,768]{2,1,0:T(8,128)(2,1)} %copy-done.7), calls=%async_computation | async-start | bytes 6291456 | tf_op jit(solution)/shard_map/all_to_all | solution.py:412
  23.4 17.4 %collective-permute-start.1 = (f32[2,2,2,64]{3,2,1,0:T(2,128)}, f32[2,2,2,64]{3,2,1,0:T(2,128)}, u32[]{:S(2)}, u32[]{:S(2)}) collective-permute-start(f32[2,2,2,64]{3,2,1,0:T(2,128)} %bitcast.27), channel_id=1, source_target_pairs={{0,2},{2,0},{4,6},{6,4},{8,10},{10,8},{12,14},{14,12},{16,18},{18,... | collective-permute-start | bytes 6152 | tf_op jit(solution)/shard_map/ppermute | solution.py:67
  41.5 5.2 collective-permute-start.2
  46.8 26.6 %collective-permute-start.3 = (f32[2,64]{1,0:T(2,128)S(1)}, f32[2,64]{1,0:T(2,128)S(1)}, u32[]{:S(2)}, u32[]{:S(2)}) collective-permute-start(f32[2,64]{1,0:T(2,128)S(1)} %bitcast.639), channel_id=1, source_target_pairs={{0,8},{2,10},{4,12},{6,14},{8,0},{10,2},{12,4},{14,6},{16,24},{18,... | collective-permute-start | bytes 1544 | tf_op jit(solution)/shard_map/ppermute | solution.py:67
  73.5 18.6 %collective-permute-start.4 = (f32[64]{0:T(128)S(1)}, f32[64]{0:T(128)S(1)}, u32[]{:S(2)}, u32[]{:S(2)}) collective-permute-start(f32[64]{0:T(128)S(1)} %fusion.171), channel_id=1, source_target_pairs={{0,16},{2,18},{4,20},{6,22},{8,24},{10,26},{12,28},{14,30},{16,0},... | collective-permute-start | bytes 776 | tf_op jit(solution)/shard_map/ppermute | solution.py:67
  92.0 1.3 collective-permute-start.5
  103.8 25.7 %collective-permute-start.6 = (bf16[2048,768]{1,0:T(8,128)(2,1)}, bf16[2048,768]{1,0:T(8,128)(2,1)}, u32[]{:S(2)}, u32[]{:S(2)}) collective-permute-start(bf16[2048,768]{1,0:T(8,128)(2,1)} %fusion.30), channel_id=1, source_target_pairs={{0,1},{1,0},{2,3},{3,2},{4,5},{5,4},{6,7},{7,6},{8,9},{9,8},{10,11... | collective-permute-start | bytes 9437192 | tf_op jit(solution)/shard_map/ppermute | solution.py:50
  106.0 9.8 %collective-permute-start = (f32[512,768]{1,0:T(8,128)}, f32[512,768]{1,0:T(8,128)}, u32[]{:S(2)}, u32[]{:S(2)}) collective-permute-start(f32[512,768]{1,0:T(8,128)} %fusion.177), channel_id=1, source_target_pairs={{0,1},{1,0},{2,3},{3,2},{4,5},{5,4},{6,7},{7,6},{8,9},{9,8},{10,11... | collective-permute-start | bytes 4718600 | tf_op jit(solution)/shard_map/ppermute | solution.py:50
  141.5 4.8 collective-permute-start.7
  165.1 31.8 %collective-permute-start.54 = (bf16[2,2,2,48,512]{4,3,2,1,0:T(8,128)(2,1)S(1)}, bf16[2,2,2,48,512]{4,3,2,1,0:T(8,128)(2,1)S(1)}, u32[]{:S(2)}, u32[]{:S(2)}) collective-permute-start(bf16[2,2,2,48,512]{4,3,2,1,0:T(8,128)(2,1)S(1)} %dynamic-slice_bitcast_fusion.3), channel_id=1, source_target_pairs={{0,4},{2,6},{4,0},{6,2},{8,12},{10,14},{12,8},{14,10},{16,20},{18,... | collective-permute-start | bytes 1179656 | tf_op jit(solution)/shard_map/ppermute | solution.py:67
  188.7 44.3 %collective-permute-start.58 = (bf16[2,2,2,48,1024]{4,3,0,1,2:T(8,128)(2,1)S(1)}, bf16[2,2,2,48,1024]{4,3,0,1,2:T(8,128)(2,1)S(1)}, u32[]{:S(2)}, u32[]{:S(2)}) collective-permute-start(bf16[2,2,2,48,1024]{4,3,0,1,2:T(8,128)(2,1)S(1)} %bitcast.625), channel_id=1, source_target_pairs={{0,8},{2,10},{4,12},{6,14},{8,0},{10,2},{12,4},{14,6},{16,24},{18,... | collective-permute-start | bytes 2359304 | tf_op jit(solution)/shard_map/ppermute | solution.py:67
  188.9 15.8 %collective-permute-start.50 = (bf16[2,2,2,48,512]{4,3,0,2,1:T(8,128)(2,1)S(1)}, bf16[2,2,2,48,512]{4,3,0,2,1:T(8,128)(2,1)S(1)}, u32[]{:S(2)}, u32[]{:S(2)}) collective-permute-start(bf16[2,2,2,48,512]{4,3,0,2,1:T(8,128)(2,1)S(1)} %bitcast.628), channel_id=1, source_target_pairs={{0,4},{2,6},{4,0},{6,2},{8,12},{10,14},{12,8},{14,10},{16,20},{18,... | collective-permute-start | bytes 1179656 | tf_op jit(solution)/shard_map/ppermute | solution.py:67
  191.5 41.9 %collective-permute-start.46 = (bf16[2,2,2,48,1024]{4,3,0,1,2:T(8,128)(2,1)S(1)}, bf16[2,2,2,48,1024]{4,3,0,1,2:T(8,128)(2,1)S(1)}, u32[]{:S(2)}, u32[]{:S(2)}) collective-permute-start(bf16[2,2,2,48,1024]{4,3,0,1,2:T(8,128)(2,1)S(1)} %bitcast.626), channel_id=1, source_target_pairs={{0,2},{2,0},{4,6},{6,4},{8,10},{10,8},{12,14},{14,12},{16,18},{18,... | collective-permute-start | bytes 2359304 | tf_op jit(solution)/shard_map/ppermute | solution.py:67
  192.7 66.3 %collective-permute-start.9 = (f32[512,768]{1,0:T(8,128)S(1)}, f32[512,768]{1,0:T(8,128)S(1)}, u32[]{:S(2)}, u32[]{:S(2)}) collective-permute-start(f32[512,768]{1,0:T(8,128)S(1)} %copy-done.29), channel_id=1, source_target_pairs={{0,1},{1,0},{2,3},{3,2},{4,5},{5,4},{6,7},{7,6},{8,9},{9,8},{10,11... | collective-permute-start | bytes 4718600 | tf_op jit(solution)/shard_map/ppermute | solution.py:50
  196.9 62.7 %collective-permute-start.8 = (f32[512,768]{1,0:T(8,128)S(1)}, f32[512,768]{1,0:T(8,128)S(1)}, u32[]{:S(2)}, u32[]{:S(2)}) collective-permute-start(f32[512,768]{1,0:T(8,128)S(1)} %copy-done.44), channel_id=1, source_target_pairs={{0,1},{1,0},{2,3},{3,2},{4,5},{5,4},{6,7},{7,6},{8,9},{9,8},{10,11... | collective-permute-start | bytes 4718600 | tf_op jit(solution)/shard_map/ppermute | solution.py:50
  204.7 7.5 %collective-permute-start.55 = (bf16[2,2,48,512]{3,2,1,0:T(8,128)(2,1)S(1)}, bf16[2,2,48,512]{3,2,1,0:T(8,128)(2,1)S(1)}, u32[]{:S(2)}, u32[]{:S(2)}) collective-permute-start(bf16[2,2,48,512]{3,2,1,0:T(8,128)(2,1)S(1)} %dynamic-slice_bitcast_fusion.8), channel_id=1, source_target_pairs={{0,8},{2,10},{4,12},{6,14},{8,0},{10,2},{12,4},{14,6},{16,24},{18,... | collective-permute-start | bytes 589832 | tf_op jit(solution)/shard_map/ppermute | solution.py:67
  212.2 5.8 %collective-permute-start.51 = (bf16[2,2,48,512]{3,2,0,1:T(8,128)(2,1)S(1)}, bf16[2,2,48,512]{3,2,0,1:T(8,128)(2,1)S(1)}, u32[]{:S(2)}, u32[]{:S(2)}) collective-permute-start(bf16[2,2,48,512]{3,2,0,1:T(8,128)(2,1)S(1)} %dynamic-slice_bitcast_fusion.9), channel_id=1, source_target_pairs={{0,8},{2,10},{4,12},{6,14},{8,0},{10,2},{12,4},{14,6},{16,24},{18,... | collective-permute-start | bytes 589832 | tf_op jit(solution)/shard_map/ppermute | solution.py:67
  218.0 5.1 collective-permute-start.56
  223.1 4.6 collective-permute-start.52
  227.8 5.2 collective-permute-start.57
  233.0 5.0 collective-permute-start.53
  233.4 7.8 %collective-permute-start.59 = (bf16[2,2,48,1024]{3,2,0,1:T(8,128)(2,1)S(1)}, bf16[2,2,48,1024]{3,2,0,1:T(8,128)(2,1)S(1)}, u32[]{:S(2)}, u32[]{:S(2)}) collective-permute-start(bf16[2,2,48,1024]{3,2,0,1:T(8,128)(2,1)S(1)} %dynamic-slice_bitcast_fusion.2), channel_id=1, source_target_pairs={{0,2},{2,0},{4,6},{6,4},{8,10},{10,8},{12,14},{14,12},{16,18},{18,... | collective-permute-start | bytes 1179656 | tf_op jit(solution)/shard_map/ppermute | solution.py:67
  233.8 9.9 %collective-permute-start.47 = (bf16[2,2,48,1024]{3,2,0,1:T(8,128)(2,1)S(1)}, bf16[2,2,48,1024]{3,2,0,1:T(8,128)(2,1)S(1)}, u32[]{:S(2)}, u32[]{:S(2)}) collective-permute-start(bf16[2,2,48,1024]{3,2,0,1:T(8,128)(2,1)S(1)} %dynamic-slice_bitcast_fusion.4), channel_id=1, source_target_pairs={{0,4},{2,6},{4,0},{6,2},{8,12},{10,14},{12,8},{14,10},{16,20},{18,... | collective-permute-start | bytes 1179656 | tf_op jit(solution)/shard_map/ppermute | solution.py:67
  241.4 5.7 collective-permute-start.60
  244.0 6.8 %collective-permute-start.48 = (bf16[2,48,1024]{2,1,0:T(8,128)(2,1)S(1)}, bf16[2,48,1024]{2,1,0:T(8,128)(2,1)S(1)}, u32[]{:S(2)}, u32[]{:S(2)}) collective-permute-start(bf16[2,48,1024]{2,1,0:T(8,128)(2,1)S(1)} %dynamic-slice_bitcast_fusion.10), channel_id=1, source_target_pairs={{0,8},{2,10},{4,12},{6,14},{8,0},{10,2},{12,4},{14,6},{16,24},{18,... | collective-permute-start | bytes 589832 | tf_op jit(solution)/shard_map/ppermute | solution.py:67
  247.2 5.6 collective-permute-start.61
  250.8 6.6 %collective-permute-start.49 = (bf16[48,1024]{1,0:T(8,128)(2,1)S(1)}, bf16[48,1024]{1,0:T(8,128)(2,1)S(1)}, u32[]{:S(2)}, u32[]{:S(2)}) collective-permute-start(bf16[48,1024]{1,0:T(8,128)(2,1)S(1)} %dynamic-slice_bitcast_fusion.20), channel_id=1, source_target_pairs={{0,16},{2,18},{4,20},{6,22},{8,24},{10,26},{12,28},{14,30},{16,0},... | collective-permute-start | bytes 294920 | tf_op jit(solution)/shard_map/ppermute | solution.py:67
  298.0 39.8 %collective-permute-start.42 = (bf16[2,2,2,48,384]{4,3,0,1,2:T(8,128)(2,1)}, bf16[2,2,2,48,384]{4,3,0,1,2:T(8,128)(2,1)}, u32[]{:S(2)}, u32[]{:S(2)}) collective-permute-start(bf16[2,2,2,48,384]{4,3,0,1,2:T(8,128)(2,1)} %bitcast.567), channel_id=1, source_target_pairs={{0,8},{2,10},{4,12},{6,14},{8,0},{10,2},{12,4},{14,6},{16,24},{18,... | collective-permute-start | bytes 884744 | tf_op jit(solution)/shard_map/ppermute | solution.py:67
  299.7 39.6 %collective-permute-start.38 = (bf16[2,2,2,48,384]{4,3,0,1,2:T(8,128)(2,1)}, bf16[2,2,2,48,384]{4,3,0,1,2:T(8,128)(2,1)}, u32[]{:S(2)}, u32[]{:S(2)}) collective-permute-start(bf16[2,2,2,48,384]{4,3,0,1,2:T(8,128)(2,1)} %bitcast.568), channel_id=1, source_target_pairs={{0,8},{2,10},{4,12},{6,14},{8,0},{10,2},{12,4},{14,6},{16,24},{18,... | collective-permute-start | bytes 884744 | tf_op jit(solution)/shard_map/ppermute | solution.py:67
  301.5 81.6 %collective-permute-start.10 = (f32[512,768]{1,0:T(8,128)}, f32[512,768]{1,0:T(8,128)}, u32[]{:S(2)}, u32[]{:S(2)}) collective-permute-start(f32[512,768]{1,0:T(8,128)} %fusion.181), channel_id=1, source_target_pairs={{0,1},{1,0},{2,3},{3,2},{4,5},{5,4},{6,7},{7,6},{8,9},{9,8},{10,11... | collective-permute-start | bytes 4718600 | tf_op jit(solution)/shard_map/ppermute | solution.py:50
  311.9 48.4 %collective-permute-start.25 = (bf16[2,2,2,48,768]{4,3,2,1,0:T(8,128)(2,1)}, bf16[2,2,2,48,768]{4,3,2,1,0:T(8,128)(2,1)}, u32[]{:S(2)}, u32[]{:S(2)}) collective-permute-start(bf16[2,2,2,48,768]{4,3,2,1,0:T(8,128)(2,1)} %dynamic-slice_bitcast_fusion), channel_id=1, source_target_pairs={{0,2},{2,0},{4,6},{6,4},{8,10},{10,8},{12,14},{14,12},{16,18},{18,... | collective-permute-start | bytes 1769480 | tf_op jit(solution)/shard_map/ppermute | solution.py:67
  336.9 112.4 %collective-permute-start.12 = (bf16[16,128,768]{2,1,0:T(8,128)(2,1)}, bf16[16,128,768]{2,1,0:T(8,128)(2,1)}, u32[]{:S(2)}, u32[]{:S(2)}) collective-permute-start(bf16[16,128,768]{2,1,0:T(8,128)(2,1)} %get-tuple-element.45), channel_id=1, source_target_pairs={{0,1},{1,0},{2,3},{3,2},{4,5},{5,4},{6,7},{7,6},{8,9},{9,8},{10,11... | collective-permute-start | bytes 9437192 | tf_op jit(solution)/shard_map/ppermute | solution.py:50
  338.9 15.6 %collective-permute-start.43 = (bf16[2,2,48,384]{3,2,0,1:T(8,128)(2,1)S(1)}, bf16[2,2,48,384]{3,2,0,1:T(8,128)(2,1)S(1)}, u32[]{:S(2)}, u32[]{:S(2)}) collective-permute-start(bf16[2,2,48,384]{3,2,0,1:T(8,128)(2,1)S(1)} %dynamic-slice_bitcast_fusion.11), channel_id=1, source_target_pairs={{0,2},{2,0},{4,6},{6,4},{8,10},{10,8},{12,14},{14,12},{16,18},{18,... | collective-permute-start | bytes 442376 | tf_op jit(solution)/shard_map/ppermute | solution.py:67
  340.4 17.0 %collective-permute-start.39 = (bf16[2,2,48,384]{3,2,0,1:T(8,128)(2,1)S(1)}, bf16[2,2,48,384]{3,2,0,1:T(8,128)(2,1)S(1)}, u32[]{:S(2)}, u32[]{:S(2)}) collective-permute-start(bf16[2,2,48,384]{3,2,0,1:T(8,128)(2,1)S(1)} %dynamic-slice_bitcast_fusion.12), channel_id=1, source_target_pairs={{0,2},{2,0},{4,6},{6,4},{8,10},{10,8},{12,14},{14,12},{16,18},{18,... | collective-permute-start | bytes 442376 | tf_op jit(solution)/shard_map/ppermute | solution.py:67
  354.5 5.7 collective-permute-start.44
  357.5 5.7 collective-permute-start.40
  360.2 10.8 %collective-permute-start.45 = (bf16[48,384]{1,0:T(8,128)(2,1)S(1)}, bf16[48,384]{1,0:T(8,128)(2,1)S(1)}, u32[]{:S(2)}, u32[]{:S(2)}) collective-permute-start(bf16[48,384]{1,0:T(8,128)(2,1)S(1)} %dynamic-slice_bitcast_fusion.28), channel_id=1, source_target_pairs={{0,16},{2,18},{4,20},{6,22},{8,24},{10,26},{12,28},{14,30},{16,0},... | collective-permute-start | bytes 110600 | tf_op jit(solution)/shard_map/ppermute | solution.py:67
  361.6 8.4 %collective-permute-start.26 = (bf16[2,2,48,768]{3,2,1,0:T(8,128)(2,1)S(1)}, bf16[2,2,48,768]{3,2,1,0:T(8,128)(2,1)S(1)}, u32[]{:S(2)}, u32[]{:S(2)}) collective-permute-start(bf16[2,2,48,768]{3,2,1,0:T(8,128)(2,1)S(1)} %dynamic-slice_bitcast_fusion.5), channel_id=1, source_target_pairs={{0,4},{2,6},{4,0},{6,2},{8,12},{10,14},{12,8},{14,10},{16,20},{18,... | collective-permute-start | bytes 884744 | tf_op jit(solution)/shard_map/ppermute | solution.py:67
  363.3 15.6 %collective-permute-start.41 = (bf16[48,384]{1,0:T(8,128)(2,1)S(1)}, bf16[48,384]{1,0:T(8,128)(2,1)S(1)}, u32[]{:S(2)}, u32[]{:S(2)}) collective-permute-start(bf16[48,384]{1,0:T(8,128)(2,1)S(1)} %dynamic-slice_bitcast_fusion.29), channel_id=1, source_target_pairs={{0,16},{2,18},{4,20},{6,22},{8,24},{10,26},{12,28},{14,30},{16,0},... | collective-permute-start | bytes 110600 | tf_op jit(solution)/shard_map/ppermute | solution.py:67
  370.1 5.2 collective-permute-start.27
  375.4 6.4 %collective-permute-start.28 = (bf16[48,768]{1,0:T(8,128)(2,1)S(1)}, bf16[48,768]{1,0:T(8,128)(2,1)S(1)}, u32[]{:S(2)}, u32[]{:S(2)}) collective-permute-start(bf16[48,768]{1,0:T(8,128)(2,1)S(1)} %dynamic-slice_bitcast_fusion.24), channel_id=1, source_target_pairs={{0,16},{2,18},{4,20},{6,22},{8,24},{10,26},{12,28},{14,30},{16,0},... | collective-permute-start | bytes 221192 | tf_op jit(solution)/shard_map/ppermute | solution.py:67
  383.1 25.6 %collective-permute-start.29 = (bf16[48,768]{1,0:T(8,128)(2,1)}, bf16[48,768]{1,0:T(8,128)(2,1)}, u32[]{:S(2)}, u32[]{:S(2)}) collective-permute-start(bf16[48,768]{1,0:T(8,128)(2,1)} %fusion.145), channel_id=1, source_target_pairs={{0,1},{1,0},{2,3},{3,2},{4,5},{5,4},{6,7},{7,6},{8,9},{9,8},{10,11... | collective-permute-start | bytes 221192 | tf_op jit(solution)/shard_map/ppermute | solution.py:50
  398.0 9.5 %collective-permute-start.34 = (bf16[2,2,2,48,384]{4,3,0,1,2:T(8,128)(2,1)S(1)}, bf16[2,2,2,48,384]{4,3,0,1,2:T(8,128)(2,1)S(1)}, u32[]{:S(2)}, u32[]{:S(2)}) collective-permute-start(bf16[2,2,2,48,384]{4,3,0,1,2:T(8,128)(2,1)S(1)} %bitcast.630), channel_id=1, source_target_pairs={{0,8},{2,10},{4,12},{6,14},{8,0},{10,2},{12,4},{14,6},{16,24},{18,... | collective-permute-start | bytes 884744 | tf_op jit(solution)/shard_map/ppermute | solution.py:67
  401.7 22.8 %collective-permute-start.30 = (bf16[2,2,2,48,1152]{4,3,0,2,1:T(8,128)(2,1)}, bf16[2,2,2,48,1152]{4,3,0,2,1:T(8,128)(2,1)}, u32[]{:S(2)}, u32[]{:S(2)}) collective-permute-start(bf16[2,2,2,48,1152]{4,3,0,2,1:T(8,128)(2,1)} %bitcast.563), channel_id=1, source_target_pairs={{0,4},{2,6},{4,0},{6,2},{8,12},{10,14},{12,8},{14,10},{16,20},{18,... | collective-permute-start | bytes 2654216 | tf_op jit(solution)/shard_map/ppermute | solution.py:67
  408.2 5.9 %collective-permute-start.35 = (bf16[2,2,48,384]{3,2,0,1:T(8,128)(2,1)}, bf16[2,2,48,384]{3,2,0,1:T(8,128)(2,1)}, u32[]{:S(2)}, u32[]{:S(2)}) collective-permute-start(bf16[2,2,48,384]{3,2,0,1:T(8,128)(2,1)} %dynamic-slice_bitcast_fusion.13), channel_id=1, source_target_pairs={{0,2},{2,0},{4,6},{6,4},{8,10},{10,8},{12,14},{14,12},{16,18},{18,... | collective-permute-start | bytes 442376 | tf_op jit(solution)/shard_map/ppermute | solution.py:67
  415.8 14.4 %collective-permute-start.36 = (bf16[2,48,384]{2,1,0:T(8,128)(2,1)}, bf16[2,48,384]{2,1,0:T(8,128)(2,1)}, u32[]{:S(2)}, u32[]{:S(2)}) collective-permute-start(bf16[2,48,384]{2,1,0:T(8,128)(2,1)} %dynamic-slice_bitcast_fusion.23), channel_id=1, source_target_pairs={{0,4},{2,6},{4,0},{6,2},{8,12},{10,14},{12,8},{14,10},{16,20},{18,... | collective-permute-start | bytes 221192 | tf_op jit(solution)/shard_map/ppermute | solution.py:67
  426.9 12.5 %collective-permute-start.31 = (bf16[2,2,48,1152]{3,2,0,1:T(8,128)(2,1)}, bf16[2,2,48,1152]{3,2,0,1:T(8,128)(2,1)}, u32[]{:S(2)}, u32[]{:S(2)}) collective-permute-start(bf16[2,2,48,1152]{3,2,0,1:T(8,128)(2,1)} %dynamic-slice_bitcast_fusion.1), channel_id=1, source_target_pairs={{0,8},{2,10},{4,12},{6,14},{8,0},{10,2},{12,4},{14,6},{16,24},{18,... | collective-permute-start | bytes 1327112 | tf_op jit(solution)/shard_map/ppermute | solution.py:67
  429.3 34.2 %collective-permute-start.11 = (f32[512,768]{1,0:T(8,128)S(1)}, f32[512,768]{1,0:T(8,128)}, u32[]{:S(2)}, u32[]{:S(2)}) collective-permute-start(f32[512,768]{1,0:T(8,128)S(1)} %fusion.182), channel_id=1, source_target_pairs={{0,1},{1,0},{2,3},{3,2},{4,5},{5,4},{6,7},{7,6},{8,9},{9,8},{10,11... | collective-permute-start | bytes 4718600 | tf_op jit(solution)/shard_map/ppermute | solution.py:50
  431.2 10.0 %collective-permute-start.37 = (bf16[48,384]{1,0:T(8,128)(2,1)S(1)}, bf16[48,384]{1,0:T(8,128)(2,1)S(1)}, u32[]{:S(2)}, u32[]{:S(2)}) collective-permute-start(bf16[48,384]{1,0:T(8,128)(2,1)S(1)} %dynamic-slice_bitcast_fusion.30), channel_id=1, source_target_pairs={{0,16},{2,18},{4,20},{6,22},{8,24},{10,26},{12,28},{14,30},{16,0},... | collective-permute-start | bytes 110600 | tf_op jit(solution)/shard_map/ppermute | solution.py:67
  440.6 6.0 %collective-permute-start.32 = (bf16[2,48,1152]{2,1,0:T(8,128)(2,1)S(1)}, bf16[2,48,1152]{2,1,0:T(8,128)(2,1)S(1)}, u32[]{:S(2)}, u32[]{:S(2)}) collective-permute-start(bf16[2,48,1152]{2,1,0:T(8,128)(2,1)S(1)} %dynamic-slice_bitcast_fusion.6), channel_id=1, source_target_pairs={{0,2},{2,0},{4,6},{6,4},{8,10},{10,8},{12,14},{14,12},{16,18},{18,... | collective-permute-start | bytes 663560 | tf_op jit(solution)/shard_map/ppermute | solution.py:67
  447.4 120.1 %collective-permute-start.33 = (bf16[48,1152]{1,0:T(8,128)(2,1)}, bf16[48,1152]{1,0:T(8,128)(2,1)}, u32[]{:S(2)}, u32[]{:S(2)}) collective-permute-start(bf16[48,1152]{1,0:T(8,128)(2,1)} %dynamic-slice_bitcast_fusion.16), channel_id=1, source_target_pairs={{0,16},{2,18},{4,20},{6,22},{8,24},{10,26},{12,28},{14,30},{16,0},... | collective-permute-start | bytes 331784 | tf_op jit(solution)/shard_map/ppermute | solution.py:67
  465.7 1.2 collective-permute-start.13
  465.9 19.9 %collective-permute-start.14 = (f32[2,2,2,8,48]{4,3,2,1,0:T(8,128)S(1)}, f32[2,2,2,8,48]{4,3,2,1,0:T(8,128)S(1)}, u32[]{:S(2)}, u32[]{:S(2)}) collective-permute-start(f32[2,2,2,8,48]{4,3,2,1,0:T(8,128)S(1)} %dynamic-slice_bitcast_fusion.32), channel_id=1, source_target_pairs={{0,2},{2,0},{4,6},{6,4},{8,10},{10,8},{12,14},{14,12},{16,18},{18,... | collective-permute-start | bytes 36872 | tf_op jit(solution)/shard_map/ppermute | solution.py:67
  475.7 94.2 %all-to-all-start.1 = ((bf16[16,128,768]{2,1,0:T(8,128)(2,1)}), bf16[16,128,768]{2,1,0:T(8,128)(2,1)S(1)}, u32[]{:S(2)}, u32[]{:S(2)}) async-start(bf16[16,128,768]{2,1,0:T(8,128)(2,1)} %bitcast.590), calls=%async_computation.1 | async-start | bytes 6291456 | tf_op jit(solution)/shard_map/all_to_all | solution.py:543
  485.9 10.4 %collective-permute-start.15 = (f32[2,2,8,48]{3,2,1,0:T(8,128)S(1)}, f32[2,2,8,48]{3,2,1,0:T(8,128)S(1)}, u32[]{:S(2)}, u32[]{:S(2)}) collective-permute-start(f32[2,2,8,48]{3,2,1,0:T(8,128)S(1)} %fusion.151), channel_id=1, source_target_pairs={{0,4},{2,6},{4,0},{6,2},{8,12},{10,14},{12,8},{14,10},{16,20},{18,... | collective-permute-start | bytes 18440 | tf_op jit(solution)/shard_map/ppermute | solution.py:67
  487.8 47.8 %collective-permute-start.19 = (bf16[768,384]{1,0:T(8,128)(2,1)S(1)}, bf16[768,384]{1,0:T(8,128)(2,1)S(1)}, u32[]{:S(2)}, u32[]{:S(2)}) collective-permute-start(bf16[768,384]{1,0:T(8,128)(2,1)S(1)} %dynamic-slice_convert_fusion), channel_id=1, source_target_pairs={{0,1},{1,0},{2,3},{3,2},{4,5},{5,4},{6,7},{7,6},{8,9},{9,8},{10,11... | collective-permute-start | bytes 1769480 | tf_op jit(solution)/shard_map/ppermute | solution.py:50
  496.3 35.9 %collective-permute-start.16 = (f32[2,8,48]{2,1,0:T(8,128)S(1)}, f32[2,8,48]{2,1,0:T(8,128)S(1)}, u32[]{:S(2)}, u32[]{:S(2)}) collective-permute-start(f32[2,8,48]{2,1,0:T(8,128)S(1)} %fusion.154), channel_id=1, source_target_pairs={{0,8},{2,10},{4,12},{6,14},{8,0},{10,2},{12,4},{14,6},{16,24},{18,... | collective-permute-start | bytes 9224 | tf_op jit(solution)/shard_map/ppermute | solution.py:67
  532.2 18.7 %collective-permute-start.17 = (f32[8,48]{1,0:T(8,128)S(1)}, f32[8,48]{1,0:T(8,128)S(1)}, u32[]{:S(2)}, u32[]{:S(2)}) collective-permute-start(f32[8,48]{1,0:T(8,128)S(1)} %fusion.163), channel_id=1, source_target_pairs={{0,16},{2,18},{4,20},{6,22},{8,24},{10,26},{12,28},{14,30},{16,0},... | collective-permute-start | bytes 4616 | tf_op jit(solution)/shard_map/ppermute | solution.py:67
  535.9 15.0 %collective-permute-start.20 = (bf16[2,2,2,48,384]{4,3,0,2,1:T(8,128)(2,1)S(1)}, bf16[2,2,2,48,384]{4,3,0,2,1:T(8,128)(2,1)S(1)}, u32[]{:S(2)}, u32[]{:S(2)}) collective-permute-start(bf16[2,2,2,48,384]{4,3,0,2,1:T(8,128)(2,1)S(1)} %bitcast.629), channel_id=1, source_target_pairs={{0,4},{2,6},{4,0},{6,2},{8,12},{10,14},{12,8},{14,10},{16,20},{18,... | collective-permute-start | bytes 884744 | tf_op jit(solution)/shard_map/ppermute | solution.py:67
  550.9 9.1 %collective-permute-start.18 = (f32[2,48]{1,0:T(2,128)S(1)}, f32[2,48]{1,0:T(2,128)S(1)}, u32[]{:S(2)}, u32[]{:S(2)}) collective-permute-start(f32[2,48]{1,0:T(2,128)S(1)} %slice.93), channel_id=1, source_target_pairs={{0,1},{1,0},{2,3},{3,2},{4,5},{5,4},{6,7},{7,6},{8,9},{9,8},{10,11... | collective-permute-start | bytes 1160 | tf_op jit(solution)/shard_map/ppermute | solution.py:50
  551.0 6.3 %collective-permute-start.21 = (bf16[2,2,48,384]{3,2,0,1:T(8,128)(2,1)S(1)}, bf16[2,2,48,384]{3,2,0,1:T(8,128)(2,1)S(1)}, u32[]{:S(2)}, u32[]{:S(2)}) collective-permute-start(bf16[2,2,48,384]{3,2,0,1:T(8,128)(2,1)S(1)} %dynamic-slice_bitcast_fusion.15), channel_id=1, source_target_pairs={{0,8},{2,10},{4,12},{6,14},{8,0},{10,2},{12,4},{14,6},{16,24},{18,... | collective-permute-start | bytes 442376 | tf_op jit(solution)/shard_map/ppermute | solution.py:67
  557.4 4.9 collective-permute-start.22
  562.3 5.1 collective-permute-start.23
  567.4 1.7 collective-permute-start.24
  (107 other events, 920.5 us)
